TPU v7x, 256 devices: a whole 4x4x8 slice. The times are simulated.
256 devices in a mesh: ctx: 64 (over x, z, core), tp: 4 (over y).
Axes of the slice: x: 4, y: 4, z: 8, core: 2. Of those that a mesh axis runs over, the one named last changes fastest.
Arguments:
- queries: bfloat16 [8192, 4096], P('ctx', 'tp'), may hold values from -6 to 6
- key_vectors: bfloat16 [8192, 4096], P('ctx', 'tp'), may hold values from -6 to 6
- stream_gate: bfloat16 [8192, 4096], P('ctx', 'tp'), may hold values from -15 to 15
- stream_key: bfloat16 [8192, 4096], P('ctx', 'tp'), may hold values from -6 to 6
- stream_value: bfloat16 [8192, 4096], P('ctx', 'tp'), may hold values from -6 to 6
- short_filter: float32 [3, 3, 4096], P(None, None, 'tp'), may hold values from -3 to 3
- long_filter: float32 [4096, 8192], P('tp', 'ctx'), may hold values from -1 to 1
- skip_gain: float32 [4096], P('tp'), may hold values from 0.3 to 1
- out_gain: float32 [4096], P('tp'), may hold values from 0.25 to 1.75
Outputs:
- hyena_out: bfloat16 [8192, 4096], P('ctx', 'tp')
- attn_out: bfloat16 [8192, 4096], P('ctx', 'tp')
All inputs are finite; a program needn't handle non-finite values.
Results may differ from a plain program's by a relative error of at most 0.024.
Values may be sent and summed in bfloat16 or wider, within the bound.
A program may use at most 64 MiB of HBM per device.

v0:
```python
import math

import jax
import jax.numpy as jnp
from jax import lax
from jax.sharding import PartitionSpec as P

DH = 128
HC = 4096


precise = lax.Precision.HIGH


def from_behind(x, axis, by):
    size = lax.axis_size(axis)
    pairs = [(i, i + by) for i in range(size) if 0 <= i + by < size]
    return lax.ppermute(x, axis, pairs)


def featurize(stream, earlier, tap_weights):
    joined = jnp.concatenate([earlier, stream], axis=0).astype(jnp.float32)
    length = stream.shape[0]
    mixed_sum = (
        tap_weights[0] * joined[2:]
        + tap_weights[1] * joined[1 : length + 1]
        + tap_weights[2] * joined[:length]
    )
    return mixed_sum.astype(jnp.bfloat16)


def angle_table(first_len, second_len, period):
    indices = (
        lax.iota(jnp.int32, first_len)[:, None] * lax.iota(jnp.int32, second_len)[None, :] % period
    )
    angles = indices.astype(jnp.float32) * (2.0 * math.pi / period)
    return (jnp.cos(angles), jnp.sin(angles))


def dft_tables(length):
    period = 2 * length
    inner_len = 1
    while 4 * inner_len * inner_len <= period and length % (2 * inner_len) == 0:
        inner_len *= 2
    outer_len = period // inner_len
    return (
        angle_table(outer_len, outer_len // 2, outer_len),
        angle_table(outer_len, inner_len, period),
        angle_table(inner_len, inner_len, inner_len),
        outer_len,
        inner_len,
    )


def split_table(table):
    upper = table.astype(jnp.bfloat16)
    lower = (table - upper.astype(jnp.float32)).astype(jnp.bfloat16)
    return (upper, lower)


def first_section(table, signal):
    if signal.dtype == jnp.bfloat16:
        upper, lower = split_table(table)
        return jnp.einsum(
            "kn,cnm->ckm", upper, signal, preferred_element_type=jnp.float32
        ) + jnp.einsum("kn,cnm->ckm", lower, signal, preferred_element_type=jnp.float32)
    return jnp.einsum("kn,cnm->ckm", table, signal, precision=precise)


def forward_dft(signal, tables):
    (outer_cos, outer_sin), (twist_cos, twist_sin), (inner_cos, inner_sin), outer_len, inner_len = (
        tables
    )
    first_re = first_section(outer_cos, signal)
    first_im = -first_section(outer_sin, signal)
    turned_re = first_re * twist_cos + first_im * twist_sin
    turned_im = first_im * twist_cos - first_re * twist_sin
    spec_re = jnp.einsum("ckn,nj->ckj", turned_re, inner_cos, precision=precise) + jnp.einsum(
        "ckn,nj->ckj", turned_im, inner_sin, precision=precise
    )
    spec_im = jnp.einsum("ckn,nj->ckj", turned_im, inner_cos, precision=precise) - jnp.einsum(
        "ckn,nj->ckj", turned_re, inner_sin, precision=precise
    )
    return (spec_re, spec_im)


def inverse_dft(spec_re, spec_im, tables):
    (outer_cos, outer_sin), (twist_cos, twist_sin), (inner_cos, inner_sin), outer_len, inner_len = (
        tables
    )
    mid_re = jnp.einsum("ckj,jn->ckn", spec_re, inner_cos, precision=precise) - jnp.einsum(
        "ckj,jn->ckn", spec_im, inner_sin, precision=precise
    )
    mid_im = jnp.einsum("ckj,jn->ckn", spec_re, inner_sin, precision=precise) + jnp.einsum(
        "ckj,jn->ckn", spec_im, inner_cos, precision=precise
    )
    back_re = mid_re * twist_cos - mid_im * twist_sin
    back_im = mid_re * twist_sin + mid_im * twist_cos
    result = jnp.einsum("kn,ckm->cnm", outer_cos, back_re, precision=precise) - jnp.einsum(
        "kn,ckm->cnm", outer_sin, back_im, precision=precise
    )
    return result / (outer_len * inner_len)


def convolve(signal, response, tables):
    channel_count, length = signal.shape
    outer_len, inner_len = (tables[3], tables[4])
    sig_re, sig_im = forward_dft(signal.reshape(channel_count, outer_len // 2, inner_len), tables)
    res_re, res_im = forward_dft(response.reshape(channel_count, outer_len // 2, inner_len), tables)
    prod_re = sig_re * res_re - sig_im * res_im
    prod_im = sig_re * res_im + sig_im * res_re
    return inverse_dft(prod_re, prod_im, tables).reshape(channel_count, length)


def to_groups(array, groups, depth_size):
    tok_rows = array.shape[0]
    heads_here = array.shape[1] // depth_size
    piece_rows = tok_rows // groups
    regrouped = array.reshape(groups, piece_rows, heads_here, depth_size).transpose(2, 0, 1, 3)
    return regrouped.reshape(groups * heads_here, piece_rows, depth_size)


def attend_block(query_block, query_pos, kv_blocks, head_size):
    block_rows = query_block.shape[0]
    key_block = kv_blocks.shape[1]

    def advance(state_carry, operands):
        run_max, run_sum, accumulated = state_carry
        kv_block, key_start = operands
        scores = jnp.einsum(
            "qd,kd->qk", query_block, kv_block[:, :head_size], preferred_element_type=jnp.float32
        ) / jnp.sqrt(jnp.float32(head_size))
        key_pos = key_start + lax.iota(jnp.int32, key_block)
        visible = key_pos[None, :] <= query_pos[:, None]
        block_max = jnp.max(jnp.where(visible, scores, -1e30), axis=1)
        new_max = jnp.maximum(run_max, block_max)
        exp_terms = jnp.where(visible, jnp.exp(scores - new_max[:, None]), 0.0)
        factor = jnp.exp(run_max - new_max)
        run_sum = factor * run_sum + jnp.sum(exp_terms, axis=1)
        accumulated = factor[:, None] * accumulated + jnp.dot(
            exp_terms.astype(jnp.bfloat16),
            kv_block[:, head_size:],
            preferred_element_type=jnp.float32,
        )
        return ((new_max, run_sum, accumulated), None)

    starts = lax.iota(jnp.int32, kv_blocks.shape[0]) * key_block
    initial = (
        jnp.full((block_rows,), -1e30, jnp.float32),
        jnp.zeros((block_rows,), jnp.float32),
        jnp.zeros((block_rows, head_size), jnp.float32),
    )
    (run_max, run_sum, accumulated), unused = lax.scan(advance, initial, (kv_blocks, starts))
    return (accumulated / run_sum[:, None]).astype(jnp.bfloat16)


def shards(
    queries,
    key_vectors,
    stream_gate,
    stream_key,
    stream_value,
    short_filter,
    long_filter,
    skip_gain,
    out_gain,
):
    tok_rows, width_here = stream_gate.shape
    ctx_count = lax.axis_size("ctx")
    length = tok_rows * ctx_count
    tail_rows = jnp.stack([stream_gate[-2:], stream_key[-2:], stream_value[-2:]])
    earlier = from_behind(tail_rows, "ctx", 1)
    gate_feat = featurize(stream_gate, earlier[0], short_filter[0])
    key_feat = featurize(stream_key, earlier[1], short_filter[1])
    value_feat = featurize(stream_value, earlier[2], short_filter[2])
    product = (key_feat.astype(jnp.float32) * value_feat.astype(jnp.float32)).astype(jnp.bfloat16)
    response = lax.all_to_all(
        long_filter.astype(jnp.bfloat16), "ctx", split_axis=0, concat_axis=1, tiled=True
    ).astype(long_filter.dtype)
    tables = dft_tables(length)
    arrived = lax.all_to_all(product.T, "ctx", split_axis=0, concat_axis=1, tiled=True)
    convolved = convolve(arrived, response, tables)
    returned = (
        lax.all_to_all(
            convolved.astype(jnp.bfloat16), "ctx", split_axis=1, concat_axis=0, tiled=True
        )
        .astype(convolved.dtype)
        .T
    )
    hyena_out = (
        gate_feat.astype(jnp.float32) * (returned + skip_gain * product.astype(jnp.float32))
    ).astype(jnp.bfloat16)
    head_size = DH
    heads_here = width_here // head_size
    group_size = ctx_count // heads_here
    piece_rows = tok_rows // group_size
    query_all = lax.all_to_all(
        to_groups(queries, group_size, head_size), "ctx", split_axis=0, concat_axis=1, tiled=True
    ).reshape(ctx_count * piece_rows, head_size)
    kv_local = jnp.concatenate(
        [
            key_vectors.reshape(tok_rows, heads_here, head_size),
            hyena_out.reshape(tok_rows, heads_here, head_size),
        ],
        axis=2,
    )
    copies = jnp.repeat(kv_local.transpose(1, 0, 2), group_size, axis=0)
    all_kv = lax.all_to_all(copies, "ctx", split_axis=0, concat_axis=1, tiled=True).reshape(
        length, 2 * head_size
    )
    sub_index = lax.axis_index("ctx") % group_size
    query_total = ctx_count * piece_rows
    row_ids = lax.iota(jnp.int32, query_total)
    query_pos = row_ids // piece_rows * tok_rows + sub_index * piece_rows + row_ids % piece_rows
    query_block = min(512, query_total)
    key_block = min(1024, length)
    pieces_out = []
    for block_index in range(query_total // query_block):
        last_source = ((block_index + 1) * query_block - 1) // piece_rows
        reach_keys = (last_source + 1) * tok_rows
        key_count = -(-reach_keys // key_block)
        kv_blocks = all_kv[: key_count * key_block].reshape(key_count, key_block, 2 * head_size)
        row_start = block_index * query_block
        pieces_out.append(
            attend_block(
                query_all[row_start : row_start + query_block],
                query_pos[row_start : row_start + query_block],
                kv_blocks,
                head_size,
            )
        )
    attended = jnp.concatenate(pieces_out, axis=0).reshape(ctx_count, piece_rows, head_size)
    homed = lax.all_to_all(attended, "ctx", split_axis=0, concat_axis=0, tiled=True)
    homed = (
        homed.reshape(heads_here, group_size, piece_rows, head_size)
        .transpose(1, 2, 0, 3)
        .reshape(tok_rows, width_here)
    )
    values = homed.astype(jnp.float32)
    sums = lax.psum(jnp.sum(values * values, axis=1), "tp")
    inverse = lax.rsqrt(sums / HC + 1e-05)
    attn_out = (values * inverse[:, None] * out_gain).astype(jnp.bfloat16)
    return (hyena_out, attn_out)


def solution(mesh):
    in_specs = (
        P("ctx", "tp"),
        P("ctx", "tp"),
        P("ctx", "tp"),
        P("ctx", "tp"),
        P("ctx", "tp"),
        P(None, None, "tp"),
        P("tp", "ctx"),
        P("tp"),
        P("tp"),
    )
    out_specs = (P("ctx", "tp"), P("ctx", "tp"))
    return jax.shard_map(shards, mesh=mesh, in_specs=in_specs, out_specs=out_specs, check_vma=False)
```

profile of v0, /device:TPU:4, one launch (start us, length us, event | category | flops | bytes accessed | tf_op | source)
XLA Modules:
  0.0 336.8 jit_solution(3958219222489883094)
XLA Ops:
  2.2 1.9 collective-permute-start
  4.1 1.8 convert_element_type.201
  5.9 12.8 %all-to-all-start.1 = ((bf16[64,16,128]{2,1,0:T(8,128)(2,1)}), bf16[64,16,128]{2,1,0:T(8,128)(2,1)S(1)}, u32[]{:S(2)}, u32[]{:S(2)}) async-start(bf16[64,16,128]{2,1,0:T(8,128)(2,1)} %bitcast.27), calls=%async_computation.1 | async-start | bytes 524288 | tf_op jit(solution)/shard_map/all_to_all | solution.py:177
  22.4 2.2 multiply_convert_fusion
  24.5 5.7 %all-to-all-done.1 = bf16[64,16,128]{2,1,0:T(8,128)(2,1)S(1)} async-done(((bf16[64,16,128]{2,1,0:T(8,128)(2,1)}), bf16[64,16,128]{2,1,0:T(8,128)(2,1)S(1)}, u32[]{:S(2)}, u32[]{:S(2)}) %all-to-all-start.1) | async-done | bytes 262176 | tf_op jit(solution)/shard_map/all_to_all | solution.py:177
  30.3 6.7 %all-to-all-start = ((bf16[64,16,128]{2,1,0:T(8,128)(2,1)}), bf16[64,16,128]{2,1,0:T(8,128)(2,1)S(1)}, u32[]{:S(2)}, u32[]{:S(2)}) async-start(bf16[64,16,128]{2,1,0:T(8,128)(2,1)} %bitcast.16), calls=%async_computation | async-start | bytes 524288 | tf_op jit(solution)/shard_map/all_to_all | solution.py:181
  41.6 6.7 %all-to-all-done = bf16[64,16,128]{2,1,0:T(8,128)(2,1)S(1)} async-done(((bf16[64,16,128]{2,1,0:T(8,128)(2,1)}), bf16[64,16,128]{2,1,0:T(8,128)(2,1)S(1)}, u32[]{:S(2)}, u32[]{:S(2)}) %all-to-all-start) | async-done | bytes 262176 | tf_op jit(solution)/shard_map/all_to_all | solution.py:181
  61.5 6.5 %all-to-all-start.2 = ((bf16[16,64,128]{2,0,1:T(8,128)(2,1)}), bf16[16,64,128]{2,0,1:T(8,128)(2,1)S(1)}, u32[]{:S(2)}, u32[]{:S(2)}) async-start(bf16[16,64,128]{2,0,1:T(8,128)(2,1)} %copy.122), calls=%async_computation.2 | async-start | bytes 524288 | tf_op jit(solution)/shard_map/all_to_all | solution.py:184
  69.4 10.1 %all-to-all-done.2 = bf16[16,64,128]{2,0,1:T(8,128)(2,1)S(1)} async-done(((bf16[16,64,128]{2,0,1:T(8,128)(2,1)}), bf16[16,64,128]{2,0,1:T(8,128)(2,1)S(1)}, u32[]{:S(2)}, u32[]{:S(2)}) %all-to-all-start.2) | async-done | bytes 262176 | tf_op jit(solution)/shard_map/all_to_all | solution.py:184
  79.6 6.5 %all-to-all-start.4 = ((bf16[64,16,128]{2,1,0:T(8,128)(2,1)}), bf16[64,16,128]{2,1,0:T(8,128)(2,1)S(1)}, u32[]{:S(2)}, u32[]{:S(2)}) async-start(bf16[64,16,128]{2,1,0:T(8,128)(2,1)} %bitcast.42), calls=%async_computation.4 | async-start | bytes 524288 | tf_op jit(solution)/shard_map/all_to_all | solution.py:197
  86.3 1.9 fusion.61
  88.5 9.1 %all-to-all-done.4 = bf16[64,16,128]{2,1,0:T(8,128)(2,1)S(1)} async-done(((bf16[64,16,128]{2,1,0:T(8,128)(2,1)}), bf16[64,16,128]{2,1,0:T(8,128)(2,1)S(1)}, u32[]{:S(2)}, u32[]{:S(2)}) %all-to-all-start.4) | async-done | bytes 262176 | tf_op jit(solution)/shard_map/all_to_all | solution.py:197
  97.6 2.5 broadcast_in_dim.14
  100.1 6.7 %all-to-all-start.3 = ((bf16[64,128,256]{2,1,0:T(8,128)(2,1)}), bf16[64,128,256]{2,1,0:T(8,128)(2,1)}, u32[]{:S(2)}, u32[]{:S(2)}) async-start(bf16[64,128,256]{2,1,0:T(8,128)(2,1)} %bitcast.203), calls=%async_computation.3 | async-start | bytes 8388608 | tf_op jit(solution)/shard_map/all_to_all | solution.py:208
  109.1 90.6 %all-to-all-done.3 = bf16[64,128,256]{2,1,0:T(8,128)(2,1)} async-done(((bf16[64,128,256]{2,1,0:T(8,128)(2,1)}), bf16[64,128,256]{2,1,0:T(8,128)(2,1)}, u32[]{:S(2)}, u32[]{:S(2)}) %all-to-all-start.3) | async-done | bytes 4194336 | tf_op jit(solution)/shard_map/all_to_all | solution.py:208
  199.7 75.9 %while.31 = (s32[]{:T(128)}, f32[512]{0:T(512)S(1)}, f32[512]{0:T(512)}, f32[512,128]{1,0:T(8,128)S(1)}, s32[8]{0:T(128)}, /*index=5*/s32[512]{0:T(512)}, bf16[8...) while((s32[]{:T(128)}, f32[512]{0:T(512)S(1)}, f32[512]{0:T(512)}, ...), condition=%wide.region_7.8_spmd.clone, body=%wide.region_4.7_spmd.clone.sunk | while | flops 275975680 | bytes 8575117 | solution.py:153
  202.7 2.0 fusion.275
  207.2 1.4 convolution_add_fusion.10
  211.6 2.0 fusion.275
  216.7 1.4 convolution_add_fusion.10
  221.2 2.0 fusion.275
  226.3 1.4 convolution_add_fusion.10
  230.8 2.0 fusion.275
  240.4 2.0 fusion.275
  249.9 2.0 fusion.275
  259.5 2.0 fusion.275
  269.1 2.0 fusion.275
  275.6 3.1 slice.180
  278.7 23.8 %while.30 = (s32[]{:T(128)}, f32[512]{0:T(512)S(1)}, f32[512]{0:T(512)S(1)}, f32[512,128]{1,0:T(8,128)S(1)}, s32[4]{0:T(128)}, /*index=5*/s32[512]{0:T(512)S(1)}...) while((s32[]{:T(128)}, f32[512]{0:T(512)S(1)}, ...), condition=%wide.region_3.4_spmd.clone, body=%wide.region_0.3_spmd.clone.sunk | while | flops 275975680 | bytes 8575117 | solution.py:153
  304.3 8.7 %all-to-all-start.5 = ((bf16[64,16,128]{2,1,0:T(8,128)(2,1)}), bf16[64,16,128]{2,1,0:T(8,128)(2,1)S(1)}, u32[]{:S(2)}, u32[]{:S(2)}) async-start(bf16[64,16,128]{2,1,0:T(8,128)(2,1)} %bitcast.46), calls=%async_computation.5 | async-start | bytes 524288 | tf_op jit(solution)/shard_map/all_to_all | solution.py:233
  313.8 10.7 %all-to-all-done.5 = bf16[64,16,128]{2,1,0:T(8,128)(2,1)S(1)} async-done(((bf16[64,16,128]{2,1,0:T(8,128)(2,1)}), bf16[64,16,128]{2,1,0:T(8,128)(2,1)S(1)}, u32[]{:S(2)}, u32[]{:S(2)}) %all-to-all-start.5) | async-done | bytes 262176 | tf_op jit(solution)/shard_map/all_to_all | solution.py:233
  325.2 10.7 %psum.7 = f32[128]{0:T(128)S(1)} all-reduce(f32[128]{0:T(128)S(1)} %reduce_sum.39), channel_id=1, replica_groups=mesh['ctx'=64,'tp'=4] {'tp'}, use_global_device_ids=true, to_apply=%region_10.11 | all-reduce | flops 128 | bytes 1024 | tf_op jit(solution)/shard_map/psum | solution.py:240
  (178 shorter events, 110.5 us)
Async XLA Ops:
  0.6 20.4 %copy-start = (bf16[128,1024]{1,0:T(8,128)(2,1)S(1)}, bf16[128,1024]{1,0:T(8,128)(2,1)}, u32[]{:S(2)}) copy-start(bf16[128,1024]{1,0:T(8,128)(2,1)} %param.17) | copy-start | bytes 786436
  2.2 19.2 %collective-permute-start = (bf16[3,2,1024]{2,1,0:T(2,128)(2,1)S(1)}, bf16[3,2,1024]{2,1,0:T(2,128)(2,1)S(1)}, u32[]{:S(2)}, u32[]{:S(2)}) collective-permute-start(bf16[3,2,1024]{2,1,0:T(2,128)(2,1)S(1)} %pad_maximum_fusion.1), channel_id=1, source_target_pairs={{0,4},{4,8},{8,12},{12,16},{16,20},{20,24},{24,28},{28,32},{32,36}... | collective-permute-start | bytes 36872 | tf_op jit(solution)/shard_map/ppermute | solution.py:18
  5.9 24.4 %all-to-all-start.1 = ((bf16[64,16,128]{2,1,0:T(8,128)(2,1)}), bf16[64,16,128]{2,1,0:T(8,128)(2,1)S(1)}, u32[]{:S(2)}, u32[]{:S(2)}) async-start(bf16[64,16,128]{2,1,0:T(8,128)(2,1)} %bitcast.27), calls=%async_computation.1 | async-start | bytes 524288 | tf_op jit(solution)/shard_map/all_to_all | solution.py:177
  30.3 18.0 %all-to-all-start = ((bf16[64,16,128]{2,1,0:T(8,128)(2,1)}), bf16[64,16,128]{2,1,0:T(8,128)(2,1)S(1)}, u32[]{:S(2)}, u32[]{:S(2)}) async-start(bf16[64,16,128]{2,1,0:T(8,128)(2,1)} %bitcast.16), calls=%async_computation | async-start | bytes 524288 | tf_op jit(solution)/shard_map/all_to_all | solution.py:181
  59.8 8.2 %copy-start.1 = (bf16[128,1024]{1,0:T(8,128)(2,1)S(1)}, bf16[128,1024]{1,0:T(8,128)(2,1)}, u32[]{:S(2)}) copy-start(bf16[128,1024]{1,0:T(8,128)(2,1)} %param.15) | copy-start | bytes 786436
  59.8 8.4 %copy-start.2 = (bf16[128,1024]{1,0:T(8,128)(2,1)S(1)}, bf16[128,1024]{1,0:T(8,128)(2,1)}, u32[]{:S(2)}) copy-start(bf16[128,1024]{1,0:T(8,128)(2,1)} %param.14) | copy-start | bytes 786436
  59.8 8.6 %copy-start.3 = (bf16[128,1024]{1,0:T(8,128)(2,1)S(1)}, bf16[128,1024]{1,0:T(8,128)(2,1)}, u32[]{:S(2)}) copy-start(bf16[128,1024]{1,0:T(8,128)(2,1)} %param.13) | copy-start | bytes 786436
  61.5 18.0 %all-to-all-start.2 = ((bf16[16,64,128]{2,0,1:T(8,128)(2,1)}), bf16[16,64,128]{2,0,1:T(8,128)(2,1)S(1)}, u32[]{:S(2)}, u32[]{:S(2)}) async-start(bf16[16,64,128]{2,0,1:T(8,128)(2,1)} %copy.122), calls=%async_computation.2 | async-start | bytes 524288 | tf_op jit(solution)/shard_map/all_to_all | solution.py:184
  68.4 17.9 %copy-start.5 = (f32[1024]{0:T(1024)S(1)}, f32[1024]{0:T(1024)}, u32[]{:S(2)}) copy-start(f32[1024]{0:T(1024)} %param.20) | copy-start | bytes 12292
  79.6 18.0 %all-to-all-start.4 = ((bf16[64,16,128]{2,1,0:T(8,128)(2,1)}), bf16[64,16,128]{2,1,0:T(8,128)(2,1)S(1)}, u32[]{:S(2)}, u32[]{:S(2)}) async-start(bf16[64,16,128]{2,1,0:T(8,128)(2,1)} %bitcast.42), calls=%async_computation.4 | async-start | bytes 524288 | tf_op jit(solution)/shard_map/all_to_all | solution.py:197
  100.1 99.6 %all-to-all-start.3 = ((bf16[64,128,256]{2,1,0:T(8,128)(2,1)}), bf16[64,128,256]{2,1,0:T(8,128)(2,1)}, u32[]{:S(2)}, u32[]{:S(2)}) async-start(bf16[64,128,256]{2,1,0:T(8,128)(2,1)} %bitcast.203), calls=%async_computation.3 | async-start | bytes 8388608 | tf_op jit(solution)/shard_map/all_to_all | solution.py:208
  275.6 3.1 copy-start.4
  303.4 32.5 %copy-start.6 = (f32[1024]{0:T(1024)S(1)}, f32[1024]{0:T(1024)}, u32[]{:S(2)}) copy-start(f32[1024]{0:T(1024)} %param.21) | copy-start | bytes 12292
  304.3 20.2 %all-to-all-start.5 = ((bf16[64,16,128]{2,1,0:T(8,128)(2,1)}), bf16[64,16,128]{2,1,0:T(8,128)(2,1)S(1)}, u32[]{:S(2)}, u32[]{:S(2)}) async-start(bf16[64,16,128]{2,1,0:T(8,128)(2,1)} %bitcast.46), calls=%async_computation.5 | async-start | bytes 524288 | tf_op jit(solution)/shard_map/all_to_all | solution.py:233
where the time goes:
time: 339 us; the launch traced here: 337 us
  waiting for transfers between devices  133 us (39%)
  matrix products  50.8 us (15%)
  starting transfers between devices  49.7 us (15%)
  other arithmetic  48.2 us (14%)
  local copies, waits for them, and re-layouts  42.7 us (13%)
  blocking collectives  10.7 us (3%)
    all_to_all x1, waiting for transfers between devices, shards(): lax.all_to_all(copies, 'ctx', split_axis=0, concat_axis=1, tiled=True)  90.6 us
    dot_general x12, matrix products, advance(): jnp.einsum('qd,kd->qk', query_block, kv_block[:, :head_size], preferred_e...  19.8 us
    dynamic_slice x12, local copies, waits for them, and re-layouts, attend_block(): lax.scan(advance, initial, (kv_blocks, starts))  14.8 us
    dot_general x12, matrix products, advance(): jnp.dot(exp_terms.astype(jnp.bfloat16), kv_block[:, head_size:], preferre...  14.2 us
    squeeze x12, local copies, waits for them, and re-layouts, attend_block(): lax.scan(advance, initial, (kv_blocks, starts))  13 us
    all_to_all x1, starting transfers between devices, shards(): lax.all_to_all(long_filter.astype(jnp.bfloat16), 'ctx', split_axis=0, con...  12.8 us
    reduce_sum x12, other arithmetic, advance(): run_sum = factor * run_sum + jnp.sum(exp_terms, axis=1)  11.5 us
    psum x1, blocking collectives, shards(): sums = lax.psum(jnp.sum(values * values, axis=1), 'tp')  10.7 us
  transfers between devices with their start and end apart: 7, of which 6 were waited for; matrix products, arithmetic and copies ran while one was open for 6% of the time, Pallas kernels for 0%

commit v1 on v0

v1 whole, which is shorter than its diff:
```python
import math

import jax
import jax.numpy as jnp
import numpy as np
from jax import lax
from jax.experimental import pallas as pl
from jax.experimental.pallas import tpu as pltpu
from jax.sharding import PartitionSpec as P

DH = 128
HC = 4096
NC = 64
TOK = 128
PIECE = 16
F32 = jnp.float32
BF16 = jnp.bfloat16


def block_of(dev):
    return (dev // 2) % 8 * 8 + dev // 16 * 2 + dev % 2


def slot_of(dev):
    return dev % 2 * 32 + dev // 2


def dft_constants():
    slots = np.arange(NC)
    first = (2 * (slots % 32) + slots // 32).astype(np.float64)
    freq = np.arange(NC) + 0.25
    inner = np.arange(TOK)
    outer = 2 * np.pi * freq[:, None] * first[None, :] / NC
    turn = 2 * np.pi * freq[:, None] * inner[None, :] / (NC * TOK)
    mix = 2 * np.pi * (inner[:, None] * inner[None, :] % TOK) / TOK
    cos, sin = np.cos(mix), np.sin(mix)
    outer_in = np.concatenate([np.cos(outer), np.sin(outer)], axis=0)
    outer_out = np.concatenate([np.cos(outer), np.sin(outer)], axis=0).T / (NC * TOK)
    inner_in = np.block([[cos, sin], [-sin, cos]])
    inner_out = np.block([[cos, -sin], [sin, cos]])
    turns = np.stack([np.cos(turn), np.sin(turn)])
    return (
        jnp.asarray(outer_in, BF16),
        jnp.asarray(turns, F32),
        jnp.asarray(inner_in, BF16),
        jnp.asarray(inner_out, BF16),
        jnp.asarray(outer_out, BF16),
    )


def rows16(index):
    return pl.ds(pl.multiple_of(index * PIECE, PIECE), PIECE)


def remote(src, dst, send_sem, recv_sem, dev):
    return pltpu.make_async_remote_copy(
        src_ref=src,
        dst_ref=dst,
        send_sem=send_sem,
        recv_sem=recv_sem,
        device_id={"ctx": dev},
        device_id_type=pl.DeviceIdType.MESH,
    )


def wait_bytes(ref, sem):
    pltpu.make_async_copy(ref, ref, sem).wait()


def mix_taps(stream, halo, taps, which, cols):
    values = stream[:, cols].astype(F32)
    behind = halo[which, :, cols].astype(F32)
    row = lax.broadcasted_iota(jnp.int32, values.shape, 0)
    once = jnp.where(row == 0, behind[15:16], pltpu.roll(values, 1, 0))
    twice = pltpu.roll(values, 2, 0)
    twice = jnp.where(row == 0, behind[14:15], jnp.where(row == 1, behind[15:16], twice))
    mixed = (
        taps[which, 0:1, cols] * values
        + taps[which, 1:2, cols] * once
        + taps[which, 2:3, cols] * twice
    )
    return mixed.astype(BF16)


def spectrum(recv, wide, half, spec, outer_in, turns, inner_in):
    wide[...] = recv[...].astype(F32)
    turn_re, turn_im = turns[0], turns[1]
    for chan in range(0, PIECE, 2):
        pair = [wide[pl.ds(chan + k, NC, stride=PIECE), :].astype(BF16) for k in range(2)]
        both = jnp.dot(outer_in[...], jnp.concatenate(pair, axis=1), preferred_element_type=F32)
        for k in range(2):
            re, im = both[:NC, k * TOK : (k + 1) * TOK], both[NC:, k * TOK : (k + 1) * TOK]
            at = pl.ds((chan + k) * NC, NC)
            half[at, 0:TOK] = (re * turn_re - im * turn_im).astype(BF16)
            half[at, TOK : 2 * TOK] = (re * turn_im + im * turn_re).astype(BF16)
    for part in range(4):
        at = pl.ds(part * 256, 256)
        spec[at, :] = jnp.dot(half[at, :], inner_in[...], preferred_element_type=F32)


def multiply_back(spec_x, spec_h, half, wide, turns, inner_out, outer_out):
    turn_re, turn_im = turns[0], turns[1]
    for part in range(4):
        at = pl.ds(part * 256, 256)
        xr, xi = spec_x[at, 0:TOK], spec_x[at, TOK : 2 * TOK]
        hr, hi = spec_h[at, 0:TOK], spec_h[at, TOK : 2 * TOK]
        half[at, 0:TOK] = (xr * hr - xi * hi).astype(BF16)
        half[at, TOK : 2 * TOK] = (xr * hi + xi * hr).astype(BF16)
    for chan in range(0, PIECE, 2):
        back = jnp.dot(
            half[pl.ds(chan * NC, 2 * NC), :], inner_out[...], preferred_element_type=F32
        )
        pair = []
        for k in range(2):
            re, im = back[k * NC : (k + 1) * NC, :TOK], back[k * NC : (k + 1) * NC, TOK:]
            turned = jnp.concatenate(
                [re * turn_re + im * turn_im, im * turn_re - re * turn_im], axis=0
            )
            pair.append(turned.astype(BF16))
        both = jnp.dot(outer_out[...], jnp.concatenate(pair, axis=1), preferred_element_type=F32)
        for k in range(2):
            wide[pl.ds(chan + k, NC, stride=PIECE), :] = both[:, k * TOK : (k + 1) * TOK]


def hyena_kernel(
    stream_gate,
    stream_key,
    stream_value,
    taps,
    long_filter,
    skip_gain,
    outer_in,
    turns,
    inner_in,
    inner_out,
    outer_out,
    out,
    halo,
    filt_send,
    prod_send,
    gate_send,
    filt_recv,
    prod_recv,
    gate_recv,
    hyena,
    home,
    wide,
    half,
    spec_x,
    spec_h,
    column,
    send_sem,
    recv_sem,
    halo_send,
    halo_recv,
):
    me = lax.axis_index("ctx")
    my_block, my_slot = block_of(me), slot_of(me)
    barrier = pltpu.get_barrier_semaphore()

    def greet(step, unused):
        pl.semaphore_signal(
            barrier,
            inc=1,
            device_id={"ctx": lax.rem(me + step, NC)},
            device_id_type=pl.DeviceIdType.MESH,
        )
        return unused

    lax.fori_loop(1, NC, greet, 0)
    filt_send[...] = long_filter[...].astype(BF16)

    @pl.when(me == 0)
    def _():
        halo[...] = jnp.zeros_like(halo)

    pl.semaphore_wait(barrier, NC - 1)

    streams = (stream_gate, stream_key, stream_value)

    @pl.when(me < NC - 1)
    def _():
        for which, stream in enumerate(streams):
            remote(
                stream.at[pl.ds(TOK - 16, 16), :],
                halo.at[which],
                halo_send.at[which],
                halo_recv.at[which],
                me + 1,
            ).start()

    def scatter(send, recv, index):
        def one(step, unused):
            dev = lax.rem(me + step, NC)
            remote(
                send.at[rows16(block_of(dev)), :],
                recv.at[rows16(my_slot), :],
                send_sem.at[index],
                recv_sem.at[index],
                dev,
            ).start()
            return unused

        lax.fori_loop(1, NC, one, 0)
        recv[rows16(my_slot), :] = send[rows16(my_block), :]

    rest = pl.ds(0, (NC - 1) * PIECE)
    scatter(filt_send, filt_recv, 0)

    @pl.when(me > 0)
    def _():
        for which in range(3):
            wait_bytes(halo.at[which], halo_recv.at[which])

    def columns(head, unused):
        cols = pl.ds(pl.multiple_of(head * DH, DH), DH)
        key_feat = mix_taps(stream_key, halo, taps, 1, cols)
        value_feat = mix_taps(stream_value, halo, taps, 2, cols)
        product = key_feat.astype(F32) * value_feat.astype(F32)
        prod_send[cols, :] = product.T.astype(BF16)
        return unused

    lax.fori_loop(0, 8, columns, 0)
    scatter(prod_send, prod_recv, 1)

    def gate_columns(head, unused):
        cols = pl.ds(pl.multiple_of(head * DH, DH), DH)
        gate_feat = mix_taps(stream_gate, halo, taps, 0, cols)
        gate_send[cols, :] = gate_feat.astype(F32).T.astype(BF16)
        return unused

    lax.fori_loop(0, 8, gate_columns, 0)
    scatter(gate_send, gate_recv, 2)

    head_row = skip_gain[pl.ds((me // 2) % 8, 1), :]
    column[...] = jnp.broadcast_to(head_row, (DH, DH)).T
    skip_tile = column[rows16(my_block % 8), :]

    wait_bytes(filt_recv.at[rest, :], recv_sem.at[0])
    spectrum(filt_recv, wide, half, spec_h, outer_in, turns, inner_in)
    wait_bytes(prod_recv.at[rest, :], recv_sem.at[1])
    spectrum(prod_recv, wide, half, spec_x, outer_in, turns, inner_in)
    multiply_back(spec_x, spec_h, half, wide, turns, inner_out, outer_out)
    wait_bytes(gate_recv.at[rest, :], recv_sem.at[2])
    skip_rows = jnp.concatenate([skip_tile] * 8, axis=0)

    def gated(part, unused):
        at = pl.ds(pl.multiple_of(part * 128, 128), 128)
        inner = wide[at, :] + skip_rows * prod_recv[at, :].astype(F32)
        hyena[at, :] = (gate_recv[at, :].astype(F32) * inner).astype(BF16)
        return unused

    lax.fori_loop(0, 8, gated, 0)

    def go_home(step, unused):
        dev = lax.rem(me + step, NC)
        remote(
            hyena.at[rows16(slot_of(dev)), :],
            home.at[rows16(my_block), :],
            send_sem.at[3],
            recv_sem.at[3],
            dev,
        ).start()
        return unused

    lax.fori_loop(1, NC, go_home, 0)
    home[rows16(my_block), :] = hyena[rows16(my_slot), :]
    wait_bytes(home.at[rest, :], recv_sem.at[3])

    def finish(head, unused):
        cols = pl.ds(pl.multiple_of(head * DH, DH), DH)
        out[:, cols] = home[cols, :].astype(F32).T.astype(BF16)
        return unused

    lax.fori_loop(0, 8, finish, 0)

    for index, send in enumerate((filt_send, prod_send, gate_send, hyena)):
        wait_bytes(send.at[rest, :], send_sem.at[index])

    @pl.when(me < NC - 1)
    def _():
        for which, stream in enumerate(streams):
            wait_bytes(stream.at[pl.ds(TOK - 16, 16), :], halo_send.at[which])


def hyena(stream_gate, stream_key, stream_value, short_filter, long_filter, skip_gain):
    vmem = pl.BlockSpec(memory_space=pltpu.VMEM)
    flat = pltpu.VMEM((NC * PIECE, TOK), BF16)
    return pl.pallas_call(
        hyena_kernel,
        out_shape=jax.ShapeDtypeStruct(stream_gate.shape, BF16),
        in_specs=[vmem] * 11,
        out_specs=vmem,
        scratch_shapes=[
            pltpu.VMEM((3, 16, 1024), BF16),
            flat, flat, flat, flat, flat, flat, flat, flat,
            pltpu.VMEM((NC * PIECE, TOK), F32),
            pltpu.VMEM((NC * PIECE, 2 * TOK), BF16),
            pltpu.VMEM((NC * PIECE, 2 * TOK), F32),
            pltpu.VMEM((NC * PIECE, 2 * TOK), F32),
            pltpu.VMEM((DH, DH), F32),
            pltpu.SemaphoreType.DMA((4,)),
            pltpu.SemaphoreType.DMA((4,)),
            pltpu.SemaphoreType.DMA((3,)),
            pltpu.SemaphoreType.DMA((3,)),
        ],
        compiler_params=pltpu.CompilerParams(
            collective_id=0, has_side_effects=True, vmem_limit_bytes=40 * 2**20
        ),
    )(
        stream_gate, stream_key, stream_value, short_filter, long_filter,
        skip_gain.reshape(8, DH), *dft_constants(),
    )


def to_groups(array, groups, depth_size):
    tok_rows = array.shape[0]
    heads_here = array.shape[1] // depth_size
    piece_rows = tok_rows // groups
    regrouped = array.reshape(groups, piece_rows, heads_here, depth_size).transpose(2, 0, 1, 3)
    return regrouped.reshape(groups * heads_here, piece_rows, depth_size)


def attend_block(query_block, query_pos, kv_blocks, head_size):
    block_rows = query_block.shape[0]
    key_block = kv_blocks.shape[1]

    def advance(state_carry, operands):
        run_max, run_sum, accumulated = state_carry
        kv_block, key_start = operands
        scores = jnp.einsum(
            "qd,kd->qk", query_block, kv_block[:, :head_size], preferred_element_type=jnp.float32
        ) / jnp.sqrt(jnp.float32(head_size))
        key_pos = key_start + lax.iota(jnp.int32, key_block)
        visible = key_pos[None, :] <= query_pos[:, None]
        block_max = jnp.max(jnp.where(visible, scores, -1e30), axis=1)
        new_max = jnp.maximum(run_max, block_max)
        exp_terms = jnp.where(visible, jnp.exp(scores - new_max[:, None]), 0.0)
        factor = jnp.exp(run_max - new_max)
        run_sum = factor * run_sum + jnp.sum(exp_terms, axis=1)
        accumulated = factor[:, None] * accumulated + jnp.dot(
            exp_terms.astype(jnp.bfloat16),
            kv_block[:, head_size:],
            preferred_element_type=jnp.float32,
        )
        return ((new_max, run_sum, accumulated), None)

    starts = lax.iota(jnp.int32, kv_blocks.shape[0]) * key_block
    initial = (
        jnp.full((block_rows,), -1e30, jnp.float32),
        jnp.zeros((block_rows,), jnp.float32),
        jnp.zeros((block_rows, head_size), jnp.float32),
    )
    (run_max, run_sum, accumulated), unused = lax.scan(advance, initial, (kv_blocks, starts))
    return (accumulated / run_sum[:, None]).astype(jnp.bfloat16)


def shards(
    queries,
    key_vectors,
    stream_gate,
    stream_key,
    stream_value,
    short_filter,
    long_filter,
    skip_gain,
    out_gain,
):
    tok_rows, width_here = stream_gate.shape
    ctx_count = lax.axis_size("ctx")
    length = tok_rows * ctx_count
    hyena_out = hyena(
        stream_gate, stream_key, stream_value, short_filter, long_filter, skip_gain
    )
    head_size = DH
    heads_here = width_here // head_size
    group_size = ctx_count // heads_here
    piece_rows = tok_rows // group_size
    query_all = lax.all_to_all(
        to_groups(queries, group_size, head_size), "ctx", split_axis=0, concat_axis=1, tiled=True
    ).reshape(ctx_count * piece_rows, head_size)
    kv_local = jnp.concatenate(
        [
            key_vectors.reshape(tok_rows, heads_here, head_size),
            hyena_out.reshape(tok_rows, heads_here, head_size),
        ],
        axis=2,
    )
    copies = jnp.repeat(kv_local.transpose(1, 0, 2), group_size, axis=0)
    all_kv = lax.all_to_all(copies, "ctx", split_axis=0, concat_axis=1, tiled=True).reshape(
        length, 2 * head_size
    )
    sub_index = lax.axis_index("ctx") % group_size
    query_total = ctx_count * piece_rows
    row_ids = lax.iota(jnp.int32, query_total)
    query_pos = row_ids // piece_rows * tok_rows + sub_index * piece_rows + row_ids % piece_rows
    query_block = min(512, query_total)
    key_block = min(1024, length)
    pieces_out = []
    for block_index in range(query_total // query_block):
        last_source = ((block_index + 1) * query_block - 1) // piece_rows
        reach_keys = (last_source + 1) * tok_rows
        key_count = -(-reach_keys // key_block)
        kv_blocks = all_kv[: key_count * key_block].reshape(key_count, key_block, 2 * head_size)
        row_start = block_index * query_block
        pieces_out.append(
            attend_block(
                query_all[row_start : row_start + query_block],
                query_pos[row_start : row_start + query_block],
                kv_blocks,
                head_size,
            )
        )
    attended = jnp.concatenate(pieces_out, axis=0).reshape(ctx_count, piece_rows, head_size)
    homed = lax.all_to_all(attended, "ctx", split_axis=0, concat_axis=0, tiled=True)
    homed = (
        homed.reshape(heads_here, group_size, piece_rows, head_size)
        .transpose(1, 2, 0, 3)
        .reshape(tok_rows, width_here)
    )
    values = homed.astype(jnp.float32)
    sums = lax.psum(jnp.sum(values * values, axis=1), "tp")
    inverse = lax.rsqrt(sums / HC + 1e-05)
    attn_out = (values * inverse[:, None] * out_gain).astype(jnp.bfloat16)
    return (hyena_out, attn_out)


def solution(mesh):
    in_specs = (
        P("ctx", "tp"),
        P("ctx", "tp"),
        P("ctx", "tp"),
        P("ctx", "tp"),
        P("ctx", "tp"),
        P(None, None, "tp"),
        P("tp", "ctx"),
        P("tp"),
        P("tp"),
    )
    out_specs = (P("ctx", "tp"), P("ctx", "tp"))
    return jax.shard_map(shards, mesh=mesh, in_specs=in_specs, out_specs=out_specs, check_vma=False)
```

time: 339 us -> 298 us (0.88)
  waiting for transfers between devices: 133 us -> 90.5 us
  Pallas kernels: 0 us -> 40.2 us
  starting transfers between devices: 49.7 us -> 20.9 us
  blocking collectives: 10.7 us -> 30.8 us
  matrix products: 50.8 us -> 33.8 us
  other arithmetic: 48.2 us -> 39.9 us
  local copies, waits for them, and re-layouts: 42.7 us -> 38 us
    pallas_call x0 -> x1, Pallas kernels: none -> 40.2 us  [hyena(): pl.pallas_call(hyena_kernel, out_shape=jax.ShapeDtypeStruct(stream_gate.s...]
    all_to_all x4 -> x0, starting transfers between devices: 34.6 us -> none  [the longest x1 12.8 us: shards(): lax.all_to_all(long_filter.astype(jnp.bfloat16), 'ctx', split_axis=0, con...]
    all_to_all x4 -> x0, waiting for transfers between devices: 33.3 us -> none  [the longest x1 10.7 us: shards(): lax.all_to_all(attended, 'ctx', split_axis=0, concat_axis=0, tiled=True)]
    all_to_all x0 -> x1, blocking collectives: none -> 20.1 us  [shards(): lax.all_to_all(attended, 'ctx', split_axis=0, concat_axis=0, tiled=True)]
    dot_general x20 -> x0, matrix products: 16.8 us -> none  [the longest x2 2.21 us: forward_dft(): jnp.einsum('ckn,nj->ckj', turned_re, inner_sin, precision=precise)]
    all_to_all x1, waiting for transfers between devices: 9.11 us -> 0.01 us  [shards(): lax.all_to_all(to_groups(queries, group_size, head_size), 'ctx', split_ax...]
    convert_element_type x6 -> x0, other arithmetic: 6.58 us -> none  [the longest x1 2.19 us: shards(): (key_feat.astype(jnp.float32) * value_feat.astype(jnp.float32)).astype(jn...]
    all_to_all x1, starting transfers between devices: 6.47 us -> 12.1 us  [shards(): lax.all_to_all(to_groups(queries, group_size, head_size), 'ctx', split_ax...]
  transfers between devices with their start and end apart: 7 -> 2, of which waited for: 6 -> 1; matrix products, arithmetic and copies ran while one was open for 6% -> 1% of each run, Pallas kernels for 0% -> 14%
where the time goes in v1:
time: 298 us; the launch traced here: 295 us
  waiting for transfers between devices  90.5 us (30%)
  Pallas kernels  40.2 us (13%)
  other arithmetic  39.9 us (13%)
  local copies, waits for them, and re-layouts  38 us (13%)
  matrix products  33.8 us (11%)
  blocking collectives  30.8 us (10%)
  starting transfers between devices  20.9 us (7%)
    all_to_all x1, waiting for transfers between devices, shards(): lax.all_to_all(copies, 'ctx', split_axis=0, concat_axis=1, tiled=True)  90.5 us
    pallas_call x1, Pallas kernels, hyena(): pl.pallas_call(hyena_kernel, out_shape=jax.ShapeDtypeStruct(stream_gate.s...  40.2 us
    all_to_all x1, blocking collectives, shards(): lax.all_to_all(attended, 'ctx', split_axis=0, concat_axis=0, tiled=True)  20.1 us
    dot_general x12, matrix products, advance(): jnp.einsum('qd,kd->qk', query_block, kv_block[:, :head_size], preferred_e...  19.7 us
    dynamic_slice x12, local copies, waits for them, and re-layouts, attend_block(): lax.scan(advance, initial, (kv_blocks, starts))  14.9 us
    dot_general x12, matrix products, advance(): jnp.dot(exp_terms.astype(jnp.bfloat16), kv_block[:, head_size:], preferre...  14 us
    squeeze x12, local copies, waits for them, and re-layouts, attend_block(): lax.scan(advance, initial, (kv_blocks, starts))  13 us
    all_to_all x1, starting transfers between devices, shards(): lax.all_to_all(to_groups(queries, group_size, head_size), 'ctx', split_ax...  12.1 us
  transfers between devices with their start and end apart: 2, of which 1 were waited for; matrix products, arithmetic and copies ran while one was open for 1% of the time, Pallas kernels for 14%

profile of v1, /device:TPU:4, one launch (start us, length us, event | category | flops | bytes accessed | tf_op | source)
XLA Modules:
  0.0 295.4 jit_solution(5440112213158142548)
XLA Ops:
  2.7 12.1 %all-to-all-start.1 = ((bf16[64,16,128]{2,1,0:T(8,128)(2,1)}), bf16[64,16,128]{2,1,0:T(8,128)(2,1)S(1)}, u32[]{:S(2)}, u32[]{:S(2)}) async-start(bf16[64,16,128]{2,1,0:T(8,128)(2,1)} %bitcast.5), calls=%async_computation.1 | async-start | bytes 524288 | tf_op jit(solution)/shard_map/all_to_all | solution.py:379
  14.9 40.2 %shard_map.149 = bf16[128,1024]{1,0:T(8,128)(2,1)S(1)} custom-call(bf16[128,1024]{1,0:T(8,128)(2,1)S(1)} %copy-done.1, bf16[128,1024]{1,0:T(8,128)(2,1)S(1)} %copy-done.2, bf16[128,1024]{1,0:T(8,128)(2,1)S(1)} %copy-done.3, f32[3,3,1024]{2,1,0:T(4,128)S(1)} %copy-done.7, f32[1024,128]{1,0:T(8,128)S(1)} %copy-done, f32[8,128]{1,0:T(8,128)S(1)} %bitcast.91, ...), custom_call_target="tpu_custom_call" | custom-call | tf_op jit(solution)/shard_map/pallas_call | solution.py:289
  55.4 2.5 broadcast_in_dim.28
  57.9 8.8 %all-to-all-start = ((bf16[64,128,256]{2,1,0:T(8,128)(2,1)}), bf16[64,128,256]{2,1,0:T(8,128)(2,1)}, u32[]{:S(2)}, u32[]{:S(2)}) async-start(bf16[64,128,256]{2,1,0:T(8,128)(2,1)} %bitcast.92), calls=%async_computation | async-start | bytes 8388608 | tf_op jit(solution)/shard_map/all_to_all | solution.py:390
  69.1 90.5 %all-to-all-done = bf16[64,128,256]{2,1,0:T(8,128)(2,1)} async-done(((bf16[64,128,256]{2,1,0:T(8,128)(2,1)}), bf16[64,128,256]{2,1,0:T(8,128)(2,1)}, u32[]{:S(2)}, u32[]{:S(2)}) %all-to-all-start) | async-done | bytes 4194336 | tf_op jit(solution)/shard_map/all_to_all | solution.py:390
  159.6 74.8 %while.31 = (s32[]{:T(128)}, f32[512]{0:T(512)S(1)}, f32[512]{0:T(512)}, f32[512,128]{1,0:T(8,128)S(1)}, s32[8]{0:T(128)}, /*index=5*/s32[512]{0:T(512)}, bf16[8...) while((s32[]{:T(128)}, f32[512]{0:T(512)S(1)}, f32[512]{0:T(512)}, ...), condition=%wide.region_7.8_spmd.clone, body=%wide.region_4.7_spmd.clone.sunk | while | flops 275975680 | bytes 8575117 | solution.py:354
  162.5 1.9 fusion.67
  166.9 1.4 convolution_add_fusion.5
  171.3 1.9 fusion.67
  175.1 1.3 fusion.69
  176.4 1.4 convolution_add_fusion.5
  180.7 1.9 fusion.67
  184.5 1.3 fusion.69
  185.8 1.4 convolution_add_fusion.5
  190.2 1.9 fusion.67
  194.0 1.3 fusion.69
  195.2 1.4 convolution_add_fusion.5
  199.6 1.9 fusion.67
  203.4 1.3 fusion.69
  204.7 1.4 convolution_add_fusion.5
  209.1 1.9 fusion.67
  212.8 1.3 fusion.69
  214.1 1.4 convolution_add_fusion.5
  218.5 1.9 fusion.67
  222.3 1.3 fusion.69
  223.6 1.4 convolution_add_fusion.5
  227.9 1.9 fusion.67
  233.0 1.4 convolution_add_fusion.5
  234.4 3.1 %slice.51 = bf16[32,128,256]{2,1,0:T(8,128)(2,1)} slice(bf16[64,128,256]{2,1,0:T(8,128)(2,1)} %all-to-all-done), slice={[0:32], [0:128], [0:256]} | slice | bytes 4194304 | tf_op jit(solution)/shard_map/slice | solution.py:404
  237.5 23.9 %while.30 = (s32[]{:T(128)}, f32[512]{0:T(512)S(1)}, f32[512]{0:T(512)S(1)}, f32[512,128]{1,0:T(8,128)S(1)}, s32[4]{0:T(128)}, /*index=5*/s32[512]{0:T(512)S(1)}...) while((s32[]{:T(128)}, f32[512]{0:T(512)S(1)}, ...), condition=%wide.region_3.4_spmd.clone, body=%wide.region_0.3_spmd.clone.sunk | while | flops 275975680 | bytes 8575117 | solution.py:354
  262.4 20.1 %all_to_all.23 = bf16[64,16,128]{2,1,0:T(8,128)(2,1)S(1)} all-to-all(bf16[64,16,128]{2,1,0:T(8,128)(2,1)S(1)} %bitcast.95), channel_id=1, replica_groups=mesh['ctx'=64,'tp'=4] {'ctx'}, dimensions={0} | all-to-all | bytes 524288 | tf_op jit(solution)/shard_map/all_to_all | solution.py:415
  283.1 10.7 %psum.7 = f32[128]{0:T(128)S(1)} all-reduce(f32[128]{0:T(128)S(1)} %reduce_sum.39), channel_id=1, replica_groups=mesh['ctx'=64,'tp'=4] {'tp'}, use_global_device_ids=true, to_apply=%region_10.11 | all-reduce | flops 128 | bytes 1024 | tf_op jit(solution)/shard_map/psum | solution.py:422
  (143 shorter events, 71.7 us)
Async XLA Ops:
  0.6 14.1 %copy-start.8 = (bf16[128,64]{1,0:T(8,128)(2,1)S(1)}, bf16[128,64]{1,0:T(8,128)(2,1)}, u32[]{:S(2)}) copy-start(bf16[128,64]{1,0:T(8,128)(2,1)} %constant.108.clone.outer_in) | copy-start | bytes 49156
  0.6 14.1 %copy-start.6 = (f32[2,64,128]{2,1,0:T(8,128)S(1)}, f32[2,64,128]{2,1,0:T(8,128)}, u32[]{:S(2)}) copy-start(f32[2,64,128]{2,1,0:T(8,128)} %constant.109.clone.turns) | copy-start | bytes 196612
  0.7 14.1 %copy-start.4 = (bf16[256,256]{1,0:T(8,128)(2,1)S(1)}, bf16[256,256]{1,0:T(8,128)(2,1)}, u32[]{:S(2)}) copy-start(bf16[256,256]{1,0:T(8,128)(2,1)} %constant.110.clone.inner_in) | copy-start | bytes 393220
  0.7 14.1 %copy-start.5 = (bf16[256,256]{1,0:T(8,128)(2,1)S(1)}, bf16[256,256]{1,0:T(8,128)(2,1)}, u32[]{:S(2)}) copy-start(bf16[256,256]{1,0:T(8,128)(2,1)} %constant.111.clone.inner_out) | copy-start | bytes 393220
  0.7 14.1 %copy-start.9 = (bf16[64,128]{1,0:T(8,128)(2,1)S(1)}, bf16[64,128]{1,0:T(8,128)(2,1)}, u32[]{:S(2)}) copy-start(bf16[64,128]{1,0:T(8,128)(2,1)} %constant.112.clone.outer_out) | copy-start | bytes 49156
  0.7 14.1 %copy-start.1 = (bf16[128,1024]{1,0:T(8,128)(2,1)S(1)}, bf16[128,1024]{1,0:T(8,128)(2,1)}, u32[]{:S(2)}) copy-start(bf16[128,1024]{1,0:T(8,128)(2,1)} %stream_gate.1) | copy-start | bytes 786436
  0.7 14.1 %copy-start.2 = (bf16[128,1024]{1,0:T(8,128)(2,1)S(1)}, bf16[128,1024]{1,0:T(8,128)(2,1)}, u32[]{:S(2)}) copy-start(bf16[128,1024]{1,0:T(8,128)(2,1)} %stream_key.1) | copy-start | bytes 786436
  0.7 14.1 %copy-start.3 = (bf16[128,1024]{1,0:T(8,128)(2,1)S(1)}, bf16[128,1024]{1,0:T(8,128)(2,1)}, u32[]{:S(2)}) copy-start(bf16[128,1024]{1,0:T(8,128)(2,1)} %stream_value.1) | copy-start | bytes 786436
  0.7 14.1 %copy-start.7 = (f32[3,3,1024]{2,1,0:T(4,128)S(1)}, f32[3,3,1024]{2,1,0:T(4,128)}, u32[]{:S(2)}) copy-start(f32[3,3,1024]{2,1,0:T(4,128)} %taps.1) | copy-start | bytes 110596
  0.7 14.1 %copy-start = (f32[1024,128]{1,0:T(8,128)S(1)}, f32[1024,128]{1,0:T(8,128)}, u32[]{:S(2)}) copy-start(f32[1024,128]{1,0:T(8,128)} %long_filter.1) | copy-start | bytes 1572868
  0.7 14.1 %copy-start.10 = (f32[1024]{0:T(1024)S(1)}, f32[1024]{0:T(1024)}, u32[]{:S(2)}) copy-start(f32[1024]{0:T(1024)} %param.25) | copy-start | bytes 12292
  1.9 53.3 %copy-start.11 = (bf16[128,1024]{1,0:T(8,128)(2,1)S(1)}, bf16[128,1024]{1,0:T(8,128)(2,1)}, u32[]{:S(2)}) copy-start(bf16[128,1024]{1,0:T(8,128)(2,1)} %param.19) | copy-start | bytes 786436
  2.7 52.7 %all-to-all-start.1 = ((bf16[64,16,128]{2,1,0:T(8,128)(2,1)}), bf16[64,16,128]{2,1,0:T(8,128)(2,1)S(1)}, u32[]{:S(2)}, u32[]{:S(2)}) async-start(bf16[64,16,128]{2,1,0:T(8,128)(2,1)} %bitcast.5), calls=%async_computation.1 | async-start | bytes 524288 | tf_op jit(solution)/shard_map/all_to_all | solution.py:379
  57.9 101.7 %all-to-all-start = ((bf16[64,128,256]{2,1,0:T(8,128)(2,1)}), bf16[64,128,256]{2,1,0:T(8,128)(2,1)}, u32[]{:S(2)}, u32[]{:S(2)}) async-start(bf16[64,128,256]{2,1,0:T(8,128)(2,1)} %bitcast.92), calls=%async_computation | async-start | bytes 8388608 | tf_op jit(solution)/shard_map/all_to_all | solution.py:390
  234.4 3.1 %copy-start.12 = (f32[512]{0:T(512)S(1)}, f32[512]{0:T(512)}, u32[]{:S(2)}) copy-start(f32[512]{0:T(512)} %custom-call.1) | copy-start | bytes 6148
  261.5 32.4 %copy-start.13 = (f32[1024]{0:T(1024)S(1)}, f32[1024]{0:T(1024)}, u32[]{:S(2)}) copy-start(f32[1024]{0:T(1024)} %param.26) | copy-start | bytes 12292

commit v2 on v1

v2 whole, which is shorter than its diff:
```python
import math

import jax
import jax.numpy as jnp
import numpy as np
from jax import lax
from jax.experimental import pallas as pl
from jax.experimental.pallas import tpu as pltpu
from jax.sharding import PartitionSpec as P

DH = 128
HC = 4096
NC = 64
TOK = 128
PIECE = 16
F32 = jnp.float32
BF16 = jnp.bfloat16
SPAN = 512
QB = 256
LOW = -1e30
SCALE = math.log2(math.e) / math.sqrt(DH)


def block_of(dev):
    return (dev // 2) % 8 * 8 + dev // 16 * 2 + dev % 2


def slot_of(dev):
    return dev % 2 * 32 + dev // 2


def dft_constants():
    slots = np.arange(NC)
    first = (2 * (slots % 32) + slots // 32).astype(np.float64)
    freq = np.arange(NC) + 0.25
    inner = np.arange(TOK)
    outer = 2 * np.pi * freq[:, None] * first[None, :] / NC
    turn = 2 * np.pi * freq[:, None] * inner[None, :] / (NC * TOK)
    mix = 2 * np.pi * (inner[:, None] * inner[None, :] % TOK) / TOK
    cos, sin = np.cos(mix), np.sin(mix)
    outer_in = np.concatenate([np.cos(outer), np.sin(outer)], axis=0)
    outer_out = np.concatenate([np.cos(outer), np.sin(outer)], axis=0).T / (NC * TOK)
    inner_in = np.block([[cos, sin], [-sin, cos]])
    inner_out = np.block([[cos, -sin], [sin, cos]])
    turns = np.stack([np.cos(turn), np.sin(turn)])
    return (
        jnp.asarray(outer_in, BF16),
        jnp.asarray(turns, F32),
        jnp.asarray(inner_in, BF16),
        jnp.asarray(inner_out, BF16),
        jnp.asarray(outer_out, BF16),
    )


def rows16(index):
    return pl.ds(pl.multiple_of(index * PIECE, PIECE), PIECE)


def remote(src, dst, send_sem, recv_sem, dev):
    return pltpu.make_async_remote_copy(
        src_ref=src,
        dst_ref=dst,
        send_sem=send_sem,
        recv_sem=recv_sem,
        device_id={"ctx": dev},
        device_id_type=pl.DeviceIdType.MESH,
    )


def remote_tp(src, dst, send_sem, recv_sem, dev):
    return pltpu.make_async_remote_copy(
        src_ref=src,
        dst_ref=dst,
        send_sem=send_sem,
        recv_sem=recv_sem,
        device_id={"tp": dev},
        device_id_type=pl.DeviceIdType.MESH,
    )


def wait_bytes(ref, sem):
    pltpu.make_async_copy(ref, ref, sem).wait()


def mix_taps(stream, halo, taps, which, cols):
    values = stream[:, cols].astype(F32)
    behind = halo[which, :, cols].astype(F32)
    row = lax.broadcasted_iota(jnp.int32, values.shape, 0)
    once = jnp.where(row == 0, behind[15:16], pltpu.roll(values, 1, 0))
    twice = pltpu.roll(values, 2, 0)
    twice = jnp.where(row == 0, behind[14:15], jnp.where(row == 1, behind[15:16], twice))
    mixed = (
        taps[which, 0:1, cols] * values
        + taps[which, 1:2, cols] * once
        + taps[which, 2:3, cols] * twice
    )
    return mixed.astype(BF16)


def spectrum(recv, wide, half, spec, outer_in, turns, inner_in):
    wide[...] = recv[...].astype(F32)
    turn_re, turn_im = turns[0], turns[1]
    for chan in range(0, PIECE, 2):
        pair = [wide[pl.ds(chan + k, NC, stride=PIECE), :].astype(BF16) for k in range(2)]
        both = jnp.dot(outer_in[...], jnp.concatenate(pair, axis=1), preferred_element_type=F32)
        for k in range(2):
            re, im = both[:NC, k * TOK : (k + 1) * TOK], both[NC:, k * TOK : (k + 1) * TOK]
            at = pl.ds((chan + k) * NC, NC)
            half[at, 0:TOK] = (re * turn_re - im * turn_im).astype(BF16)
            half[at, TOK : 2 * TOK] = (re * turn_im + im * turn_re).astype(BF16)
    for part in range(4):
        at = pl.ds(part * 256, 256)
        spec[at, :] = jnp.dot(half[at, :], inner_in[...], preferred_element_type=F32)


def multiply_back(spec_x, spec_h, half, wide, turns, inner_out, outer_out):
    turn_re, turn_im = turns[0], turns[1]
    for part in range(4):
        at = pl.ds(part * 256, 256)
        xr, xi = spec_x[at, 0:TOK], spec_x[at, TOK : 2 * TOK]
        hr, hi = spec_h[at, 0:TOK], spec_h[at, TOK : 2 * TOK]
        half[at, 0:TOK] = (xr * hr - xi * hi).astype(BF16)
        half[at, TOK : 2 * TOK] = (xr * hi + xi * hr).astype(BF16)
    for chan in range(0, PIECE, 2):
        back = jnp.dot(
            half[pl.ds(chan * NC, 2 * NC), :], inner_out[...], preferred_element_type=F32
        )
        pair = []
        for k in range(2):
            re, im = back[k * NC : (k + 1) * NC, :TOK], back[k * NC : (k + 1) * NC, TOK:]
            turned = jnp.concatenate(
                [re * turn_re + im * turn_im, im * turn_re - re * turn_im], axis=0
            )
            pair.append(turned.astype(BF16))
        both = jnp.dot(outer_out[...], jnp.concatenate(pair, axis=1), preferred_element_type=F32)
        for k in range(2):
            wide[pl.ds(chan + k, NC, stride=PIECE), :] = both[:, k * TOK : (k + 1) * TOK]


def attend_scores(
    block, core, across, queries, keys, scores, weights, stats
):
    own = queries[pl.ds(pl.multiple_of(core * 1024 + block * 128, 128), 128), :]
    other = queries[pl.ds(pl.multiple_of((1 - core) * 1024 + block * 128, 128), 128), :]
    both = jnp.concatenate([own, other], axis=0)

    def chunk_rows(chunk):
        return pl.ds(pl.multiple_of(chunk * SPAN, SPAN), SPAN)

    def chunk_scores(chunk):
        return lax.dot_general(
            keys[chunk_rows(chunk), :],
            both,
            (((1,), (1,)), ((), ())),
            preferred_element_type=F32,
        )

    def first(chunk, run_max):
        here = chunk_scores(chunk)
        scores[chunk_rows(chunk), :] = here
        return jnp.maximum(run_max, here.reshape(SPAN // 8, 8, QB).max(axis=0))

    run_max = lax.fori_loop(0, block, first, jnp.full((8, QB), LOW, F32))
    row = lax.broadcasted_iota(jnp.int32, (SPAN, QB), 0)
    lane = lax.broadcasted_iota(jnp.int32, (SPAN, QB), 1)
    key_pos = row // 128 * 256 + core * 128 + row % 128
    parity = jnp.where(lane < 128, core, 1 - core)
    query_pos = lane % 128 // 32 * 256 + parity * 128 + across * 32 + lane % 32
    here = jnp.where(key_pos <= query_pos, chunk_scores(block), LOW)
    scores[chunk_rows(block), :] = here
    run_max = jnp.maximum(run_max, here.reshape(SPAN // 8, 8, QB).max(axis=0))
    top = run_max.max(axis=0, keepdims=True) * SCALE
    base = block * (block + 1) // 2

    def second(chunk, total):
        terms = jnp.exp2(scores[chunk_rows(chunk), :] * SCALE - top)
        weights[chunk_rows(base + chunk), :] = terms.astype(BF16)
        return total + terms.reshape(SPAN // 8, 8, QB).sum(axis=0)

    total = lax.fori_loop(0, block + 1, second, jnp.zeros((8, QB), F32))
    stats[pl.ds(block, 1), :] = top
    stats[pl.ds(8 + block, 1), :] = total.sum(axis=0, keepdims=True)


def attend_values(block, values, weights, stats, other_stats):
    base = block * (block + 1) // 2

    def one(chunk, total):
        lanes = pl.ds(pl.multiple_of(chunk * SPAN, SPAN), SPAN)
        rows = pl.ds(pl.multiple_of((base + chunk) * SPAN, SPAN), SPAN)
        return total + jnp.dot(
            values[:, lanes], weights[rows, :], preferred_element_type=F32
        )

    total = lax.fori_loop(0, block + 1, one, jnp.zeros((DH, QB), F32))
    top, count = stats[pl.ds(block, 1), :], stats[pl.ds(8 + block, 1), :]
    swap = lambda v: jnp.concatenate([v[:, 128:], v[:, :128]], axis=1)
    other_top = swap(other_stats[pl.ds(block, 1), :])
    other_count = swap(other_stats[pl.ds(8 + block, 1), :])
    both_top = jnp.maximum(top, other_top)
    mine = jnp.exp2(top - both_top)
    whole = mine * count + jnp.exp2(other_top - both_top) * other_count
    return total * (mine / whole)


def kernel(
    queries, key_vectors, stream_gate, stream_key, stream_value,
    taps, long_filter, skip_gain, out_gain,
    outer_in, turns, inner_in, inner_out, outer_out,
    hyena_out, attn_out,
    halo, filt_send, prod_send, gate_send, filt_recv, prod_recv, gate_recv,
    hyena, home, wide, half, spec_x, spec_h, column,
    query_all, key_all, value_all, scores, weights, stats, other_stats,
    own_part, part_send, part_recv, att_send, att_home, squares,
    send_sem, recv_sem, halo_send, halo_recv, part_out, part_in,
):
    me = lax.axis_index("ctx")
    tp = lax.axis_index("tp")
    across, depth, core = me // 16, (me // 2) % 8, me % 2
    pair, sibling = me // 2, me + 1 - 2 * core
    member = across * 2 + core
    my_block, my_slot = block_of(me), slot_of(me)
    barrier = pltpu.get_barrier_semaphore()

    def greet(step, unused):
        pl.semaphore_signal(
            barrier,
            inc=1,
            device_id={"ctx": lax.rem(me + step, NC)},
            device_id_type=pl.DeviceIdType.MESH,
        )
        return unused

    lax.fori_loop(1, NC, greet, 0)
    for step in range(1, 4):
        pl.semaphore_signal(
            barrier,
            inc=1,
            device_id={"tp": lax.rem(tp + step, 4)},
            device_id_type=pl.DeviceIdType.MESH,
        )
    filt_send[...] = long_filter[...].astype(BF16)

    @pl.when(me == 0)
    def _():
        halo[...] = jnp.zeros_like(halo)

    pl.semaphore_wait(barrier, NC - 1 + 3)

    streams = (stream_gate, stream_key, stream_value)

    @pl.when(me < NC - 1)
    def _():
        for which, stream in enumerate(streams):
            remote(
                stream.at[pl.ds(TOK - 16, 16), :],
                halo.at[which],
                halo_send.at[which],
                halo_recv.at[which],
                me + 1,
            ).start()

    def scatter(send, recv, index):
        def one(step, unused):
            dev = lax.rem(me + step, NC)
            remote(
                send.at[rows16(block_of(dev)), :],
                recv.at[rows16(my_slot), :],
                send_sem.at[index],
                recv_sem.at[index],
                dev,
            ).start()
            return unused

        lax.fori_loop(1, NC, one, 0)
        recv[rows16(my_slot), :] = send[rows16(my_block), :]

    rest = pl.ds(0, (NC - 1) * PIECE)
    scatter(filt_send, filt_recv, 0)

    @pl.when(me > 0)
    def _():
        for which in range(3):
            wait_bytes(halo.at[which], halo_recv.at[which])

    def columns(head, unused):
        cols = pl.ds(pl.multiple_of(head * DH, DH), DH)
        key_feat = mix_taps(stream_key, halo, taps, 1, cols)
        value_feat = mix_taps(stream_value, halo, taps, 2, cols)
        product = key_feat.astype(F32) * value_feat.astype(F32)
        prod_send[cols, :] = product.T.astype(BF16)
        return unused

    lax.fori_loop(0, 8, columns, 0)
    scatter(prod_send, prod_recv, 1)

    key_rows = pl.ds(pl.multiple_of(pair * 128, 128), 128)

    def key_out(step, unused):
        head = lax.rem(depth + step, 8)
        remote(
            key_vectors.at[:, pl.ds(pl.multiple_of(head * DH, DH), DH)],
            key_all.at[key_rows, :],
            send_sem.at[4],
            recv_sem.at[4],
            across * 16 + head * 2 + core,
        ).start()
        return unused

    lax.fori_loop(1, 8, key_out, 0)
    my_cols = pl.ds(pl.multiple_of(depth * DH, DH), DH)
    key_all[key_rows, :] = key_vectors[:, my_cols]

    query_rows = pl.ds(pl.multiple_of(core * 1024 + pair * 32, 32), 32)

    def query_out(step, unused):
        goal = lax.rem(pair + step, 32)
        remote(
            queries.at[
                pl.ds(pl.multiple_of(goal // 8 * 32, 32), 32),
                pl.ds(pl.multiple_of(goal % 8 * DH, DH), DH),
            ],
            query_all.at[query_rows, :],
            send_sem.at[5],
            recv_sem.at[5],
            goal * 2 + core,
        ).start()
        return unused

    lax.fori_loop(1, 32, query_out, 0)
    across_rows = pl.ds(pl.multiple_of(across * 32, 32), 32)
    query_all[query_rows, :] = queries[across_rows, my_cols]

    def gate_columns(head, unused):
        cols = pl.ds(pl.multiple_of(head * DH, DH), DH)
        gate_feat = mix_taps(stream_gate, halo, taps, 0, cols)
        gate_send[cols, :] = gate_feat.astype(F32).T.astype(BF16)
        return unused

    lax.fori_loop(0, 8, gate_columns, 0)
    scatter(gate_send, gate_recv, 2)

    head_row = skip_gain[pl.ds(depth, 1), :]
    column[...] = jnp.broadcast_to(head_row, (DH, DH)).T
    skip_tile = column[rows16(my_block % 8), :]

    wait_bytes(filt_recv.at[rest, :], recv_sem.at[0])
    spectrum(filt_recv, wide, half, spec_h, outer_in, turns, inner_in)
    wait_bytes(prod_recv.at[rest, :], recv_sem.at[1])

    wait_bytes(key_all.at[pl.ds(0, 7 * 128), :], recv_sem.at[4])
    keys_here = pl.ds(pl.multiple_of(across * 1024, 1024), 1024)

    def key_on(step, unused):
        remote(
            key_all.at[keys_here, :],
            key_all.at[keys_here, :],
            send_sem.at[6],
            recv_sem.at[6],
            lax.rem(across + step, 4) * 16 + depth * 2 + core,
        ).start()
        return unused

    lax.fori_loop(1, 4, key_on, 0)
    wait_bytes(query_all.at[pl.ds(0, 31 * 32), :], recv_sem.at[5])
    queries_here = pl.ds(pl.multiple_of(core * 1024, 1024), 1024)
    query_on = remote(
        query_all.at[queries_here, :],
        query_all.at[queries_here, :],
        send_sem.at[7],
        recv_sem.at[7],
        sibling,
    )
    query_on.start()

    spectrum(prod_recv, wide, half, spec_x, outer_in, turns, inner_in)
    multiply_back(spec_x, spec_h, half, wide, turns, inner_out, outer_out)
    wait_bytes(gate_recv.at[rest, :], recv_sem.at[2])

    def gated(slot, unused):
        at = rows16(slot)
        inner = wide[at, :] + skip_tile * prod_recv[at, :].astype(F32)
        lanes = pl.ds(pl.multiple_of(slot * TOK, TOK), TOK)
        hyena[:, lanes] = (gate_recv[at, :].astype(F32) * inner).astype(BF16)
        return unused

    lax.fori_loop(0, NC, gated, 0)

    def value_out(step, unused):
        goal = lax.rem(member + step, 8)
        remote(
            hyena.at[:, pl.ds(pl.multiple_of(goal % 2 * 4096, 4096), 4096)],
            value_all.at[rows16(member), :],
            send_sem.at[8],
            recv_sem.at[8],
            goal // 2 * 16 + depth * 2 + goal % 2,
        ).start()
        return unused

    lax.fori_loop(1, 8, value_out, 0)
    value_all[rows16(member), :] = hyena[:, pl.ds(pl.multiple_of(core * 4096, 4096), 4096)]

    def go_home(step, unused):
        dev = lax.rem(me + step, NC)
        remote(
            hyena.at[:, pl.ds(pl.multiple_of(slot_of(dev) * TOK, TOK), TOK)],
            home.at[rows16(my_block), :],
            send_sem.at[3],
            recv_sem.at[3],
            dev,
        ).start()
        return unused

    lax.fori_loop(1, NC, go_home, 0)
    home[rows16(my_block), :] = hyena[:, pl.ds(pl.multiple_of(my_slot * TOK, TOK), TOK)]

    wait_bytes(key_all.at[pl.ds(0, 3 * 1024), :], recv_sem.at[6])
    query_on.wait_recv()

    def scoring(step, unused):
        block = lax.rem(depth + step, 8)
        attend_scores(
            block, core, across, query_all, key_all, scores, weights, stats
        )
        return unused

    lax.fori_loop(0, 8, scoring, 0)
    stats_out = remote(stats, other_stats, send_sem.at[9], recv_sem.at[9], sibling)
    stats_out.start()

    wait_bytes(home.at[rest, :], recv_sem.at[3])

    def finish(head, unused):
        cols = pl.ds(pl.multiple_of(head * DH, DH), DH)
        hyena_out[:, cols] = home[cols, :].astype(F32).T.astype(BF16)
        return unused

    lax.fori_loop(0, 8, finish, 0)

    stats_out.wait_recv()
    wait_bytes(value_all.at[pl.ds(0, 7 * PIECE), :], recv_sem.at[8])

    def part_copy(block):
        return remote(
            part_send.at[block],
            part_recv.at[block],
            part_out.at[block],
            part_in.at[block],
            sibling,
        )

    def settle(block):
        part_copy(block).wait_recv()
        whole = own_part[block] + part_recv[block].astype(F32)
        att_send[pl.ds(pl.multiple_of(block * 128, 128), 128), :] = whole.T.astype(BF16)

        for k in range(4):
            goal = block * 4 + k
            rows = pl.ds(pl.multiple_of(goal * 32, 32), 32)

            @pl.when(goal != pair)
            def _():
                remote(
                    att_send.at[rows, :],
                    att_home.at[across_rows, my_cols],
                    send_sem.at[10],
                    recv_sem.at[10],
                    goal * 2 + core,
                ).start()

            @pl.when(goal == pair)
            def _():
                att_home[across_rows, my_cols] = att_send[rows, :]

    def valuing(step, unused):
        block = lax.rem(depth + step, 8)
        total = attend_values(block, value_all, weights, stats, other_stats)
        own_part[block] = total[:, :128]
        part_send[block] = total[:, 128:].astype(BF16)
        part_copy(block).start()

        @pl.when(step > 0)
        def _():
            settle(lax.rem(depth + step + 7, 8))

        return unused

    lax.fori_loop(0, 8, valuing, 0)
    settle(lax.rem(depth + 7, 8))

    wait_bytes(att_send.at[pl.ds(0, 31 * 32), :], recv_sem.at[10])
    summed = jnp.zeros((TOK, DH), F32)
    for head in range(8):
        part = att_home[:, head * DH : (head + 1) * DH].astype(F32)
        summed = summed + part * part
    squares[tp] = jnp.broadcast_to(summed.T.sum(axis=0, keepdims=True), (8, TOK))
    for step in range(1, 4):
        remote_tp(
            squares.at[tp],
            squares.at[tp],
            send_sem.at[11],
            recv_sem.at[11],
            lax.rem(tp + step, 4),
        ).start()
    wait_bytes(squares.at[pl.ds(0, 3)], recv_sem.at[11])
    mean = (squares[0] + squares[1] + squares[2] + squares[3]) * (1.0 / HC)
    inverse = jnp.broadcast_to(lax.rsqrt(mean + 1e-05)[0:1, :], (TOK, TOK)).T
    for head in range(8):
        cols = slice(head * DH, (head + 1) * DH)
        part = att_home[:, cols].astype(F32)
        attn_out[:, cols] = (part * inverse * out_gain[0:1, cols]).astype(BF16)

    for index, send in enumerate((filt_send, prod_send, gate_send, home)):
        wait_bytes(send.at[rest, :], send_sem.at[index])
    wait_bytes(key_all.at[pl.ds(0, 7 * 128), :], send_sem.at[4])
    wait_bytes(query_all.at[pl.ds(0, 31 * 32), :], send_sem.at[5])
    wait_bytes(key_all.at[pl.ds(0, 3 * 1024), :], send_sem.at[6])
    query_on.wait_send()
    wait_bytes(value_all.at[pl.ds(0, 7 * PIECE), :], send_sem.at[8])
    stats_out.wait_send()
    for block in range(8):
        part_copy(block).wait_send()
    wait_bytes(att_send.at[pl.ds(0, 31 * 32), :], send_sem.at[10])
    wait_bytes(squares.at[pl.ds(0, 3)], send_sem.at[11])

    @pl.when(me < NC - 1)
    def _():
        for which, stream in enumerate(streams):
            wait_bytes(stream.at[pl.ds(TOK - 16, 16), :], halo_send.at[which])


def shards(
    queries, key_vectors, stream_gate, stream_key, stream_value,
    short_filter, long_filter, skip_gain, out_gain,
):
    vmem = pl.BlockSpec(memory_space=pltpu.VMEM)
    flat = pltpu.VMEM((NC * PIECE, TOK), BF16)
    dma = pltpu.SemaphoreType.DMA
    shape = jax.ShapeDtypeStruct(stream_gate.shape, BF16)
    return pl.pallas_call(
        kernel,
        out_shape=(shape, shape),
        in_specs=[vmem] * 14,
        out_specs=(vmem, vmem),
        scratch_shapes=[
            pltpu.VMEM((3, 16, 1024), BF16),
            flat, flat, flat, flat, flat, flat,
            pltpu.VMEM((PIECE, NC * TOK), BF16),
            flat,
            pltpu.VMEM((NC * PIECE, TOK), F32),
            pltpu.VMEM((NC * PIECE, 2 * TOK), BF16),
            pltpu.VMEM((NC * PIECE, 2 * TOK), F32),
            pltpu.VMEM((NC * PIECE, 2 * TOK), F32),
            pltpu.VMEM((DH, DH), F32),
            pltpu.VMEM((2048, DH), BF16),
            pltpu.VMEM((4096, DH), BF16),
            pltpu.VMEM((DH, 4096), BF16),
            pltpu.VMEM((4096, QB), F32),
            pltpu.VMEM((36 * SPAN, QB), BF16),
            pltpu.VMEM((16, QB), F32),
            pltpu.VMEM((16, QB), F32),
            pltpu.VMEM((8, DH, 128), F32),
            pltpu.VMEM((8, DH, 128), BF16),
            pltpu.VMEM((8, DH, 128), BF16),
            flat,
            pltpu.VMEM((TOK, 1024), BF16),
            pltpu.VMEM((4, 8, TOK), F32),
            dma((12,)), dma((12,)), dma((3,)), dma((3,)), dma((8,)), dma((8,)),
        ],
        compiler_params=pltpu.CompilerParams(
            collective_id=0, has_side_effects=True, vmem_limit_bytes=48 * 2**20
        ),
    )(
        queries, key_vectors, stream_gate, stream_key, stream_value, short_filter, long_filter,
        skip_gain.reshape(8, DH), out_gain.reshape(1, 1024), *dft_constants(),
    )


def solution(mesh):
    in_specs = (
        P("ctx", "tp"),
        P("ctx", "tp"),
        P("ctx", "tp"),
        P("ctx", "tp"),
        P("ctx", "tp"),
        P(None, None, "tp"),
        P("tp", "ctx"),
        P("tp"),
        P("tp"),
    )
    out_specs = (P("ctx", "tp"), P("ctx", "tp"))
    return jax.shard_map(shards, mesh=mesh, in_specs=in_specs, out_specs=out_specs, check_vma=False)
```

time: 298 us -> 102 us (0.34)
  waiting for transfers between devices: 90.5 us -> 0 us
  Pallas kernels: 40.2 us -> 87.1 us
  other arithmetic: 39.9 us -> 0 us
  matrix products: 33.8 us -> 0 us
  blocking collectives: 30.8 us -> 0 us
  local copies, waits for them, and re-layouts: 38 us -> 13.5 us
  starting transfers between devices: 20.9 us -> 0 us
    all_to_all x2 -> x0, waiting for transfers between devices: 90.5 us -> none  [the longest x1 90.5 us: shards(): lax.all_to_all(copies, 'ctx', split_axis=0, concat_axis=1, tiled=True)]
    pallas_call x1, Pallas kernels: 40.2 us -> 87.1 us  [shards(): pl.pallas_call(kernel, out_shape=(shape, shape), in_specs=[vmem] * 14, ou...]
    dot_general x24 -> x0, matrix products: 33.8 us -> none  [the longest x12 19.7 us: advance(): jnp.einsum('qd,kd->qk', query_block, kv_block[:, :head_size], preferred_e...]
    all_to_all x2 -> x0, starting transfers between devices: 20.9 us -> none  [the longest x1 12.1 us: shards(): lax.all_to_all(to_groups(queries, group_size, head_size), 'ctx', split_ax...]
    all_to_all x1 -> x0, blocking collectives: 20.1 us -> none  [shards(): lax.all_to_all(attended, 'ctx', split_axis=0, concat_axis=0, tiled=True)]
    add x25 -> x0, other arithmetic: 17.1 us -> none  [the longest x12 9.62 us: advance(): run_sum = factor * run_sum + jnp.sum(exp_terms, axis=1)]
    dynamic_slice x12 -> x0, local copies, waits for them, and re-layouts: 14.9 us -> none  [attend_block(): lax.scan(advance, initial, (kv_blocks, starts))]
    squeeze x12 -> x0, local copies, waits for them, and re-layouts: 13 us -> none  [attend_block(): lax.scan(advance, initial, (kv_blocks, starts))]
  transfers between devices with their start and end apart: 2 -> 0, of which waited for: 1 -> 0; matrix products, arithmetic and copies ran while one was open for 1% -> 0% of each run, Pallas kernels for 14% -> 0%
where the time goes in v2:
time: 102 us; the launch traced here: 101 us
  Pallas kernels  87.1 us (85%)
  local copies, waits for them, and re-layouts  13.5 us (13%)
    pallas_call x1, Pallas kernels, shards(): pl.pallas_call(kernel, out_shape=(shape, shape), in_specs=[vmem] * 14, ou...  87.1 us
    unnamed x30, local copies, waits for them, and re-layouts  13.5 us

profile of v2, /device:TPU:4, one launch (start us, length us, event | category | flops | bytes accessed | tf_op | source)
XLA Modules:
  0.0 101.2 jit_solution(11550587572830702441)
XLA Ops:
  0.6 0.0 copy-start
  0.6 1.0 %copy-done = f32[1024,128]{1,0:T(8,128)S(1)} copy-done((f32[1024,128]{1,0:T(8,128)S(1)}, f32[1024,128]{1,0:T(8,128)}, u32[]{:S(2)}) %copy-start) | copy-done | bytes 524312
  1.7 0.0 copy-start.1
  1.7 0.9 copy-done.1
  2.6 0.0 copy-start.2
  2.6 0.9 copy-done.2
  3.6 0.0 copy-start.3
  3.6 0.9 copy-done.3
  4.5 0.0 copy-start.4
  4.5 0.9 copy-done.4
  5.5 0.0 copy-start.5
  5.5 0.9 copy-done.5
  6.4 0.0 copy-start.6
  6.4 0.9 copy-done.6
  7.3 0.0 copy-start.7
  7.3 0.9 copy-done.7
  8.2 0.0 copy-start.8
  8.2 0.8 copy-done.8
  9.1 0.0 copy-start.9
  9.1 0.8 copy-done.9
  9.9 0.0 copy-start.10
  9.9 0.8 copy-done.10
  10.6 0.0 copy-start.11
  10.6 0.7 copy-done.11
  11.4 0.0 copy-start.12
  11.4 0.7 copy-done.12
  12.0 0.0 copy-start.13
  12.0 0.7 copy-done.13
  12.7 87.1 %shard_map.149 = (bf16[128,1024]{1,0:T(8,128)(2,1)S(1)}, bf16[128,1024]{1,0:T(8,128)(2,1)S(1)}) custom-call(bf16[128,1024]{1,0:T(8,128)(2,1)S(1)} %copy-done.1, bf16[128,1024]{1,0:T(8,128)(2,1)S(1)} %copy-done.2, bf16[128,1024]{1,0:T(8,128)(2,1)S(1)} %copy-done.3, bf16[128,1024]{1,0:T(8,128)(2,1)S(1)} %copy-done.4, bf16[128,1024]{1,0:T(8,128)(2,1)S(1)} %copy-done.5, ...), custom_call_target="tpu_custom_call" | custom-call | tf_op jit(solution)/shard_map/pallas_call | solution.py:540
  99.8 0.7 copy.18
  100.5 0.7 copy.19
Async XLA Ops:
  0.6 1.0 %copy-start = (f32[1024,128]{1,0:T(8,128)S(1)}, f32[1024,128]{1,0:T(8,128)}, u32[]{:S(2)}) copy-start(f32[1024,128]{1,0:T(8,128)} %long_filter.1) | copy-start | bytes 1572868
  1.7 0.9 copy-start.1
  2.6 0.9 copy-start.2
  3.6 0.9 copy-start.3
  4.5 0.9 copy-start.4
  5.5 0.9 copy-start.5
  6.4 0.9 copy-start.6
  7.3 0.9 copy-start.7
  8.2 0.8 copy-start.8
  9.1 0.8 copy-start.9
  9.9 0.8 copy-start.10
  10.6 0.7 copy-start.11
  11.4 0.7 copy-start.12
  12.0 0.7 copy-start.13

commit v3 on v2

--- a/solution.py
+++ b/solution.py
@@ -182,17 +182,20 @@
     stats[pl.ds(8 + block, 1), :] = total.sum(axis=0, keepdims=True)
 
 
-def attend_values(block, values, weights, stats, other_stats):
-    base = block * (block + 1) // 2
-
-    def one(chunk, total):
-        lanes = pl.ds(pl.multiple_of(chunk * SPAN, SPAN), SPAN)
-        rows = pl.ds(pl.multiple_of((base + chunk) * SPAN, SPAN), SPAN)
-        return total + jnp.dot(
-            values[:, lanes], weights[rows, :], preferred_element_type=F32
-        )
-
-    total = lax.fori_loop(0, block + 1, one, jnp.zeros((DH, QB), F32))
+def value_chunk(chunk, values, weights, totals):
+    lanes = slice(chunk * 1024, (chunk + 1) * 1024)
+    for block in range(2 * chunk, 8):
+        first = (block * (block + 1) // 2 + 2 * chunk) * SPAN
+        reach = SPAN if block == 2 * chunk else 2 * SPAN
+        add = jnp.dot(
+            values[:, lanes][:, :reach],
+            weights[first : first + reach, :],
+            preferred_element_type=F32,
+        )
+        totals[block] = add if chunk == 0 else totals[block] + add
+
+
+def share_factor(block, stats, other_stats):
     top, count = stats[pl.ds(block, 1), :], stats[pl.ds(8 + block, 1), :]
     swap = lambda v: jnp.concatenate([v[:, 128:], v[:, :128]], axis=1)
     other_top = swap(other_stats[pl.ds(block, 1), :])
@@ -200,19 +203,22 @@
     both_top = jnp.maximum(top, other_top)
     mine = jnp.exp2(top - both_top)
     whole = mine * count + jnp.exp2(other_top - both_top) * other_count
-    return total * (mine / whole)
+    return mine / whole
 
 
 def kernel(
-    queries, key_vectors, stream_gate, stream_key, stream_value,
-    taps, long_filter, skip_gain, out_gain,
+    queries, key_vectors, gate_hbm, key_hbm, value_hbm,
+    taps_hbm, filter_hbm, skip_hbm, gain_hbm,
+    outer_in_hbm, turns_hbm, inner_in_hbm, inner_out_hbm, outer_out_hbm,
+    hyena_out, attn_out,
+    stream_gate, stream_key, stream_value, taps, long_filter, skip_gain, out_gain,
     outer_in, turns, inner_in, inner_out, outer_out,
-    hyena_out, attn_out,
     halo, filt_send, prod_send, gate_send, filt_recv, prod_recv, gate_recv,
     hyena, home, wide, half, spec_x, spec_h, column,
     query_all, key_all, value_all, scores, weights, stats, other_stats,
-    own_part, part_send, part_recv, att_send, att_home, squares,
+    totals, own_part, part_send, part_recv, att_send, att_home, squares,
     send_sem, recv_sem, halo_send, halo_recv, part_out, part_in,
+    load_sem, value_out_sem, value_in_sem,
 ):
     me = lax.axis_index("ctx")
     tp = lax.axis_index("tp")
@@ -239,15 +245,49 @@
             device_id={"tp": lax.rem(tp + step, 4)},
             device_id_type=pl.DeviceIdType.MESH,
         )
-    filt_send[...] = long_filter[...].astype(BF16)
+    loads = [
+        pltpu.make_async_copy(src, dst, load_sem.at[index])
+        for index, (src, dst) in enumerate(
+            (
+                (filter_hbm, long_filter),
+                (taps_hbm, taps),
+                (key_hbm, stream_key),
+                (value_hbm, stream_value),
+                (gate_hbm, stream_gate),
+                (outer_in_hbm, outer_in),
+                (turns_hbm, turns),
+                (inner_in_hbm, inner_in),
+                (inner_out_hbm, inner_out),
+                (outer_out_hbm, outer_out),
+                (skip_hbm, skip_gain),
+                (gain_hbm, out_gain),
+            )
+        )
+    ]
+    key_rows = pl.ds(pl.multiple_of(pair * 128, 128), 128)
+    query_rows = pl.ds(pl.multiple_of(core * 1024 + pair * 32, 32), 32)
+    across_rows = pl.ds(pl.multiple_of(across * 32, 32), 32)
+    my_cols = pl.ds(pl.multiple_of(depth * DH, DH), DH)
+    loads.append(
+        pltpu.make_async_copy(key_vectors.at[:, my_cols], key_all.at[key_rows, :], load_sem.at[12])
+    )
+    loads.append(
+        pltpu.make_async_copy(
+            queries.at[across_rows, my_cols], query_all.at[query_rows, :], load_sem.at[13]
+        )
+    )
+    for load in loads:
+        load.start()
 
     @pl.when(me == 0)
     def _():
         halo[...] = jnp.zeros_like(halo)
 
+    loads[0].wait()
+    filt_send[...] = long_filter[...].astype(BF16)
     pl.semaphore_wait(barrier, NC - 1 + 3)
 
-    streams = (stream_gate, stream_key, stream_value)
+    streams = (gate_hbm, key_hbm, value_hbm)
 
     @pl.when(me < NC - 1)
     def _():
@@ -259,6 +299,19 @@
                 halo_recv.at[which],
                 me + 1,
             ).start()
+
+    def key_out(step, unused):
+        head = lax.rem(depth + step, 8)
+        remote(
+            key_vectors.at[:, pl.ds(pl.multiple_of(head * DH, DH), DH)],
+            key_all.at[key_rows, :],
+            send_sem.at[4],
+            recv_sem.at[4],
+            across * 16 + head * 2 + core,
+        ).start()
+        return unused
+
+    lax.fori_loop(1, 8, key_out, 0)
 
     def scatter(send, recv, index):
         def one(step, unused):
@@ -278,6 +331,9 @@
     rest = pl.ds(0, (NC - 1) * PIECE)
     scatter(filt_send, filt_recv, 0)
 
+    for load in loads[1:5]:
+        load.wait()
+
     @pl.when(me > 0)
     def _():
         for which in range(3):
@@ -294,24 +350,14 @@
     lax.fori_loop(0, 8, columns, 0)
     scatter(prod_send, prod_recv, 1)
 
-    key_rows = pl.ds(pl.multiple_of(pair * 128, 128), 128)
-
-    def key_out(step, unused):
-        head = lax.rem(depth + step, 8)
-        remote(
-            key_vectors.at[:, pl.ds(pl.multiple_of(head * DH, DH), DH)],
-            key_all.at[key_rows, :],
-            send_sem.at[4],
-            recv_sem.at[4],
-            across * 16 + head * 2 + core,
-        ).start()
-        return unused
-
-    lax.fori_loop(1, 8, key_out, 0)
-    my_cols = pl.ds(pl.multiple_of(depth * DH, DH), DH)
-    key_all[key_rows, :] = key_vectors[:, my_cols]
-
-    query_rows = pl.ds(pl.multiple_of(core * 1024 + pair * 32, 32), 32)
+    def gate_columns(head, unused):
+        cols = pl.ds(pl.multiple_of(head * DH, DH), DH)
+        gate_feat = mix_taps(stream_gate, halo, taps, 0, cols)
+        gate_send[cols, :] = gate_feat.astype(F32).T.astype(BF16)
+        return unused
+
+    lax.fori_loop(0, 8, gate_columns, 0)
+    scatter(gate_send, gate_recv, 2)
 
     def query_out(step, unused):
         goal = lax.rem(pair + step, 32)
@@ -328,26 +374,9 @@
         return unused
 
     lax.fori_loop(1, 32, query_out, 0)
-    across_rows = pl.ds(pl.multiple_of(across * 32, 32), 32)
-    query_all[query_rows, :] = queries[across_rows, my_cols]
-
-    def gate_columns(head, unused):
-        cols = pl.ds(pl.multiple_of(head * DH, DH), DH)
-        gate_feat = mix_taps(stream_gate, halo, taps, 0, cols)
-        gate_send[cols, :] = gate_feat.astype(F32).T.astype(BF16)
-        return unused
-
-    lax.fori_loop(0, 8, gate_columns, 0)
-    scatter(gate_send, gate_recv, 2)
-
-    head_row = skip_gain[pl.ds(depth, 1), :]
-    column[...] = jnp.broadcast_to(head_row, (DH, DH)).T
-    skip_tile = column[rows16(my_block % 8), :]
-
-    wait_bytes(filt_recv.at[rest, :], recv_sem.at[0])
-    spectrum(filt_recv, wide, half, spec_h, outer_in, turns, inner_in)
-    wait_bytes(prod_recv.at[rest, :], recv_sem.at[1])
-
+
+    for load in loads[5:]:
+        load.wait()
     wait_bytes(key_all.at[pl.ds(0, 7 * 128), :], recv_sem.at[4])
     keys_here = pl.ds(pl.multiple_of(across * 1024, 1024), 1024)
 
@@ -362,16 +391,14 @@
         return unused
 
     lax.fori_loop(1, 4, key_on, 0)
-    wait_bytes(query_all.at[pl.ds(0, 31 * 32), :], recv_sem.at[5])
-    queries_here = pl.ds(pl.multiple_of(core * 1024, 1024), 1024)
-    query_on = remote(
-        query_all.at[queries_here, :],
-        query_all.at[queries_here, :],
-        send_sem.at[7],
-        recv_sem.at[7],
-        sibling,
-    )
-    query_on.start()
+
+    head_row = skip_gain[pl.ds(depth, 1), :]
+    column[...] = jnp.broadcast_to(head_row, (DH, DH)).T
+    skip_tile = column[rows16(my_block % 8), :]
+
+    wait_bytes(filt_recv.at[rest, :], recv_sem.at[0])
+    spectrum(filt_recv, wide, half, spec_h, outer_in, turns, inner_in)
+    wait_bytes(prod_recv.at[rest, :], recv_sem.at[1])
 
     spectrum(prod_recv, wide, half, spec_x, outer_in, turns, inner_in)
     multiply_back(spec_x, spec_h, half, wide, turns, inner_out, outer_out)
@@ -384,21 +411,25 @@
         hyena[:, lanes] = (gate_recv[at, :].astype(F32) * inner).astype(BF16)
         return unused
 
-    lax.fori_loop(0, NC, gated, 0)
-
-    def value_out(step, unused):
-        goal = lax.rem(member + step, 8)
-        remote(
-            hyena.at[:, pl.ds(pl.multiple_of(goal % 2 * 4096, 4096), 4096)],
-            value_all.at[rows16(member), :],
-            send_sem.at[8],
-            recv_sem.at[8],
-            goal // 2 * 16 + depth * 2 + goal % 2,
-        ).start()
-        return unused
-
-    lax.fori_loop(1, 8, value_out, 0)
-    value_all[rows16(member), :] = hyena[:, pl.ds(pl.multiple_of(core * 4096, 4096), 4096)]
+    for chunk in range(4):
+        lax.fori_loop(chunk * 8, chunk * 8 + 8, gated, 0, unroll=True)
+        lax.fori_loop(32 + chunk * 8, 32 + chunk * 8 + 8, gated, 0, unroll=True)
+
+        def value_out(step, unused):
+            goal = lax.rem(member + step, 8)
+            lanes = pl.ds(pl.multiple_of(goal % 2 * 4096 + chunk * 1024, 1024), 1024)
+            remote(
+                hyena.at[:, lanes],
+                value_all.at[rows16(member), pl.ds(chunk * 1024, 1024)],
+                value_out_sem.at[chunk],
+                value_in_sem.at[chunk],
+                goal // 2 * 16 + depth * 2 + goal % 2,
+            ).start()
+            return unused
+
+        lax.fori_loop(1, 8, value_out, 0)
+        lanes = pl.ds(pl.multiple_of(core * 4096 + chunk * 1024, 1024), 1024)
+        value_all[rows16(member), pl.ds(chunk * 1024, 1024)] = hyena[:, lanes]
 
     def go_home(step, unused):
         dev = lax.rem(me + step, NC)
@@ -414,6 +445,16 @@
     lax.fori_loop(1, NC, go_home, 0)
     home[rows16(my_block), :] = hyena[:, pl.ds(pl.multiple_of(my_slot * TOK, TOK), TOK)]
 
+    wait_bytes(query_all.at[pl.ds(0, 31 * 32), :], recv_sem.at[5])
+    queries_here = pl.ds(pl.multiple_of(core * 1024, 1024), 1024)
+    query_on = remote(
+        query_all.at[queries_here, :],
+        query_all.at[queries_here, :],
+        send_sem.at[7],
+        recv_sem.at[7],
+        sibling,
+    )
+    query_on.start()
     wait_bytes(key_all.at[pl.ds(0, 3 * 1024), :], recv_sem.at[6])
     query_on.wait_recv()
 
@@ -428,17 +469,12 @@
     stats_out = remote(stats, other_stats, send_sem.at[9], recv_sem.at[9], sibling)
     stats_out.start()
 
-    wait_bytes(home.at[rest, :], recv_sem.at[3])
-
-    def finish(head, unused):
-        cols = pl.ds(pl.multiple_of(head * DH, DH), DH)
-        hyena_out[:, cols] = home[cols, :].astype(F32).T.astype(BF16)
-        return unused
-
-    lax.fori_loop(0, 8, finish, 0)
-
+    for chunk in range(4):
+        wait_bytes(
+            value_all.at[pl.ds(0, 7 * PIECE), pl.ds(chunk * 1024, 1024)], value_in_sem.at[chunk]
+        )
+        value_chunk(chunk, value_all, weights, totals)
     stats_out.wait_recv()
-    wait_bytes(value_all.at[pl.ds(0, 7 * PIECE), :], recv_sem.at[8])
 
     def part_copy(block):
         return remote(
@@ -472,21 +508,30 @@
             def _():
                 att_home[across_rows, my_cols] = att_send[rows, :]
 
-    def valuing(step, unused):
+    def sharing(step, unused):
         block = lax.rem(depth + step, 8)
-        total = attend_values(block, value_all, weights, stats, other_stats)
+        total = totals[block] * share_factor(block, stats, other_stats)
         own_part[block] = total[:, :128]
         part_send[block] = total[:, 128:].astype(BF16)
         part_copy(block).start()
-
-        @pl.when(step > 0)
-        def _():
-            settle(lax.rem(depth + step + 7, 8))
-
-        return unused
-
-    lax.fori_loop(0, 8, valuing, 0)
-    settle(lax.rem(depth + 7, 8))
+        return unused
+
+    lax.fori_loop(0, 8, sharing, 0)
+
+    def settling(step, unused):
+        settle(lax.rem(depth + step, 8))
+        return unused
+
+    lax.fori_loop(0, 8, settling, 0)
+
+    wait_bytes(home.at[rest, :], recv_sem.at[3])
+
+    def finish(head, unused):
+        cols = pl.ds(pl.multiple_of(head * DH, DH), DH)
+        hyena_out[:, cols] = home[cols, :].astype(F32).T.astype(BF16)
+        return unused
+
+    lax.fori_loop(0, 8, finish, 0)
 
     wait_bytes(att_send.at[pl.ds(0, 31 * 32), :], recv_sem.at[10])
     summed = jnp.zeros((TOK, DH), F32)
@@ -516,7 +561,10 @@
     wait_bytes(query_all.at[pl.ds(0, 31 * 32), :], send_sem.at[5])
     wait_bytes(key_all.at[pl.ds(0, 3 * 1024), :], send_sem.at[6])
     query_on.wait_send()
-    wait_bytes(value_all.at[pl.ds(0, 7 * PIECE), :], send_sem.at[8])
+    for chunk in range(4):
+        wait_bytes(
+            value_all.at[pl.ds(0, 7 * PIECE), pl.ds(chunk * 1024, 1024)], value_out_sem.at[chunk]
+        )
     stats_out.wait_send()
     for block in range(8):
         part_copy(block).wait_send()
@@ -536,13 +584,20 @@
     vmem = pl.BlockSpec(memory_space=pltpu.VMEM)
     flat = pltpu.VMEM((NC * PIECE, TOK), BF16)
     dma = pltpu.SemaphoreType.DMA
+    constants = dft_constants()
     shape = jax.ShapeDtypeStruct(stream_gate.shape, BF16)
     return pl.pallas_call(
         kernel,
         out_shape=(shape, shape),
-        in_specs=[vmem] * 14,
+        in_specs=[pl.BlockSpec(memory_space=pltpu.HBM)] * 14,
         out_specs=(vmem, vmem),
         scratch_shapes=[
+            *[pltpu.VMEM((TOK, 1024), BF16)] * 3,
+            pltpu.VMEM((3, 3, 1024), F32),
+            pltpu.VMEM((1024, TOK), F32),
+            pltpu.VMEM((8, DH), F32),
+            pltpu.VMEM((1, 1024), F32),
+            *[pltpu.VMEM(c.shape, c.dtype) for c in constants],
             pltpu.VMEM((3, 16, 1024), BF16),
             flat, flat, flat, flat, flat, flat,
             pltpu.VMEM((PIECE, NC * TOK), BF16),
@@ -559,6 +614,7 @@
             pltpu.VMEM((36 * SPAN, QB), BF16),
             pltpu.VMEM((16, QB), F32),
             pltpu.VMEM((16, QB), F32),
+            pltpu.VMEM((8, DH, QB), F32),
             pltpu.VMEM((8, DH, 128), F32),
             pltpu.VMEM((8, DH, 128), BF16),
             pltpu.VMEM((8, DH, 128), BF16),
@@ -566,13 +622,14 @@
             pltpu.VMEM((TOK, 1024), BF16),
             pltpu.VMEM((4, 8, TOK), F32),
             dma((12,)), dma((12,)), dma((3,)), dma((3,)), dma((8,)), dma((8,)),
+            dma((14,)), dma((4,)), dma((4,)),
         ],
         compiler_params=pltpu.CompilerParams(
             collective_id=0, has_side_effects=True, vmem_limit_bytes=48 * 2**20
         ),
     )(
         queries, key_vectors, stream_gate, stream_key, stream_value, short_filter, long_filter,
-        skip_gain.reshape(8, DH), out_gain.reshape(1, 1024), *dft_constants(),
+        skip_gain.reshape(8, DH), out_gain.reshape(1, 1024), *constants,
     )
 
 

time: 102 us -> 89.2 us (0.87)
  the two profiles are of different devices: /device:TPU:4 before, /device:TPU:2 now
where the time goes in v3:
time: 89.2 us; the launch traced here: 88.6 us
  Pallas kernels  74.4 us (83%)
  local copies, waits for them, and re-layouts  13.5 us (15%)
    pallas_call x1, Pallas kernels, shards(): pl.pallas_call(kernel, out_shape=(shape, shape), in_specs=[pl.BlockSpec(m...  74.4 us
    unnamed x30, local copies, waits for them, and re-layouts  13.5 us

profile of v3, /device:TPU:2, one launch (start us, length us, event | category | flops | bytes accessed | tf_op | source)
XLA Modules:
  0.0 88.6 jit_solution(4568895135181132648)
XLA Ops:
  0.6 0.0 copy-start
  0.6 1.0 %copy-done = f32[1024,128]{1,0:T(8,128)S(1)} copy-done((f32[1024,128]{1,0:T(8,128)S(1)}, f32[1024,128]{1,0:T(8,128)}, u32[]{:S(2)}) %copy-start) | copy-done | bytes 524312
  1.7 0.0 copy-start.1
  1.7 0.9 %copy-done.1 = bf16[128,1024]{1,0:T(8,128)(2,1)S(1)} copy-done((bf16[128,1024]{1,0:T(8,128)(2,1)S(1)}, bf16[128,1024]{1,0:T(8,128)(2,1)}, u32[]{:S(2)}) %copy-start.1) | copy-done | bytes 262168
  2.6 0.0 copy-start.2
  2.6 0.9 %copy-done.2 = bf16[128,1024]{1,0:T(8,128)(2,1)S(1)} copy-done((bf16[128,1024]{1,0:T(8,128)(2,1)S(1)}, bf16[128,1024]{1,0:T(8,128)(2,1)}, u32[]{:S(2)}) %copy-start.2) | copy-done | bytes 262168
  3.6 0.0 copy-start.3
  3.6 0.9 %copy-done.3 = bf16[128,1024]{1,0:T(8,128)(2,1)S(1)} copy-done((bf16[128,1024]{1,0:T(8,128)(2,1)S(1)}, bf16[128,1024]{1,0:T(8,128)(2,1)}, u32[]{:S(2)}) %copy-start.3) | copy-done | bytes 262168
  4.5 0.0 copy-start.4
  4.5 0.9 %copy-done.4 = bf16[128,1024]{1,0:T(8,128)(2,1)S(1)} copy-done((bf16[128,1024]{1,0:T(8,128)(2,1)S(1)}, bf16[128,1024]{1,0:T(8,128)(2,1)}, u32[]{:S(2)}) %copy-start.4) | copy-done | bytes 262168
  5.5 0.0 copy-start.5
  5.5 0.9 %copy-done.5 = bf16[128,1024]{1,0:T(8,128)(2,1)S(1)} copy-done((bf16[128,1024]{1,0:T(8,128)(2,1)S(1)}, bf16[128,1024]{1,0:T(8,128)(2,1)}, u32[]{:S(2)}) %copy-start.5) | copy-done | bytes 262168
  6.4 0.0 copy-start.6
  6.4 0.9 %copy-done.6 = bf16[256,256]{1,0:T(8,128)(2,1)S(1)} copy-done((bf16[256,256]{1,0:T(8,128)(2,1)S(1)}, bf16[256,256]{1,0:T(8,128)(2,1)}, u32[]{:S(2)}) %copy-start.6) | copy-done | bytes 131096
  7.3 0.0 copy-start.7
  7.3 0.9 %copy-done.7 = bf16[256,256]{1,0:T(8,128)(2,1)S(1)} copy-done((bf16[256,256]{1,0:T(8,128)(2,1)S(1)}, bf16[256,256]{1,0:T(8,128)(2,1)}, u32[]{:S(2)}) %copy-start.7) | copy-done | bytes 131096
  8.2 0.0 copy-start.8
  8.2 0.8 copy-done.8
  9.1 0.0 copy-start.9
  9.1 0.8 copy-done.9
  9.9 0.0 copy-start.10
  9.9 0.8 copy-done.10
  10.6 0.0 copy-start.11
  10.6 0.7 copy-done.11
  11.4 0.0 copy-start.12
  11.4 0.7 copy-done.12
  12.0 0.0 copy-start.13
  12.0 0.7 copy-done.13
  12.7 74.4 %shard_map.149 = (bf16[128,1024]{1,0:T(8,128)(2,1)S(1)}, bf16[128,1024]{1,0:T(8,128)(2,1)S(1)}) custom-call(bf16[128,1024]{1,0:T(8,128)(2,1)S(1)} %copy-done.1, bf16[128,1024]{1,0:T(8,128)(2,1)S(1)} %copy-done.2, bf16[128,1024]{1,0:T(8,128)(2,1)S(1)} %copy-done.3, bf16[128,1024]{1,0:T(8,128)(2,1)S(1)} %copy-done.4, bf16[128,1024]{1,0:T(8,128)(2,1)S(1)} %copy-done.5, ...), custom_call_target="tpu_custom_call" | custom-call | tf_op jit(solution)/shard_map/pallas_call | solution.py:589
  87.2 0.7 copy.18
  87.9 0.7 copy.19
Async XLA Ops:
  0.6 1.0 %copy-start = (f32[1024,128]{1,0:T(8,128)S(1)}, f32[1024,128]{1,0:T(8,128)}, u32[]{:S(2)}) copy-start(f32[1024,128]{1,0:T(8,128)} %filter_hbm.1) | copy-start | bytes 1572868
  1.7 0.9 %copy-start.1 = (bf16[128,1024]{1,0:T(8,128)(2,1)S(1)}, bf16[128,1024]{1,0:T(8,128)(2,1)}, u32[]{:S(2)}) copy-start(bf16[128,1024]{1,0:T(8,128)(2,1)} %queries.1) | copy-start | bytes 786436
  2.6 0.9 %copy-start.2 = (bf16[128,1024]{1,0:T(8,128)(2,1)S(1)}, bf16[128,1024]{1,0:T(8,128)(2,1)}, u32[]{:S(2)}) copy-start(bf16[128,1024]{1,0:T(8,128)(2,1)} %key_vectors.1) | copy-start | bytes 786436
  3.6 0.9 %copy-start.3 = (bf16[128,1024]{1,0:T(8,128)(2,1)S(1)}, bf16[128,1024]{1,0:T(8,128)(2,1)}, u32[]{:S(2)}) copy-start(bf16[128,1024]{1,0:T(8,128)(2,1)} %gate_hbm.1) | copy-start | bytes 786436
  4.5 0.9 %copy-start.4 = (bf16[128,1024]{1,0:T(8,128)(2,1)S(1)}, bf16[128,1024]{1,0:T(8,128)(2,1)}, u32[]{:S(2)}) copy-start(bf16[128,1024]{1,0:T(8,128)(2,1)} %key_hbm.1) | copy-start | bytes 786436
  5.5 0.9 %copy-start.5 = (bf16[128,1024]{1,0:T(8,128)(2,1)S(1)}, bf16[128,1024]{1,0:T(8,128)(2,1)}, u32[]{:S(2)}) copy-start(bf16[128,1024]{1,0:T(8,128)(2,1)} %value_hbm.1) | copy-start | bytes 786436
  6.4 0.9 %copy-start.6 = (bf16[256,256]{1,0:T(8,128)(2,1)S(1)}, bf16[256,256]{1,0:T(8,128)(2,1)}, u32[]{:S(2)}) copy-start(bf16[256,256]{1,0:T(8,128)(2,1)} %constant.13.clone.inner_out_hbm) | copy-start | bytes 393220
  7.3 0.9 %copy-start.7 = (bf16[256,256]{1,0:T(8,128)(2,1)S(1)}, bf16[256,256]{1,0:T(8,128)(2,1)}, u32[]{:S(2)}) copy-start(bf16[256,256]{1,0:T(8,128)(2,1)} %constant.12.clone.inner_in_hbm) | copy-start | bytes 393220
  8.2 0.8 copy-start.8
  9.1 0.8 copy-start.9
  9.9 0.8 copy-start.10
  10.6 0.7 copy-start.11
  11.4 0.7 copy-start.12
  12.0 0.7 copy-start.13

commit v4 on v3

--- a/solution.py
+++ b/solution.py
@@ -137,49 +137,60 @@
             wide[pl.ds(chan + k, NC, stride=PIECE), :] = both[:, k * TOK : (k + 1) * TOK]
 
 
-def attend_scores(
-    block, core, across, queries, keys, scores, weights, stats
-):
-    own = queries[pl.ds(pl.multiple_of(core * 1024 + block * 128, 128), 128), :]
-    other = queries[pl.ds(pl.multiple_of((1 - core) * 1024 + block * 128, 128), 128), :]
-    both = jnp.concatenate([own, other], axis=0)
-
-    def chunk_rows(chunk):
-        return pl.ds(pl.multiple_of(chunk * SPAN, SPAN), SPAN)
-
-    def chunk_scores(chunk):
-        return lax.dot_general(
-            keys[chunk_rows(chunk), :],
-            both,
-            (((1,), (1,)), ((), ())),
-            preferred_element_type=F32,
-        )
-
-    def first(chunk, run_max):
-        here = chunk_scores(chunk)
-        scores[chunk_rows(chunk), :] = here
-        return jnp.maximum(run_max, here.reshape(SPAN // 8, 8, QB).max(axis=0))
-
-    run_max = lax.fori_loop(0, block, first, jnp.full((8, QB), LOW, F32))
+def span(chunk):
+    return pl.ds(pl.multiple_of(chunk * SPAN, SPAN), SPAN)
+
+
+def visible_bias(core, across):
     row = lax.broadcasted_iota(jnp.int32, (SPAN, QB), 0)
     lane = lax.broadcasted_iota(jnp.int32, (SPAN, QB), 1)
     key_pos = row // 128 * 256 + core * 128 + row % 128
     parity = jnp.where(lane < 128, core, 1 - core)
     query_pos = lane % 128 // 32 * 256 + parity * 128 + across * 32 + lane % 32
-    here = jnp.where(key_pos <= query_pos, chunk_scores(block), LOW)
-    scores[chunk_rows(block), :] = here
-    run_max = jnp.maximum(run_max, here.reshape(SPAN // 8, 8, QB).max(axis=0))
-    top = run_max.max(axis=0, keepdims=True) * SCALE
-    base = block * (block + 1) // 2
-
-    def second(chunk, total):
-        terms = jnp.exp2(scores[chunk_rows(chunk), :] * SCALE - top)
-        weights[chunk_rows(base + chunk), :] = terms.astype(BF16)
+    return jnp.where(key_pos <= query_pos, 0.0, LOW)
+
+
+def attend_scores(core, queries, keys, score_slots, bias, weights, stats):
+    def both_halves(block):
+        own = queries[pl.ds(pl.multiple_of(core * 1024 + block * 128, 128), 128), :]
+        other = queries[pl.ds(pl.multiple_of((1 - core) * 1024 + block * 128, 128), 128), :]
+        return jnp.concatenate([own, other], axis=0)
+
+    def score(block, chunk, run_max, masked):
+        here = lax.dot_general(
+            keys[span(chunk), :],
+            both_halves(block),
+            (((1,), (1,)), ((), ())),
+            preferred_element_type=F32,
+        )
+        if masked:
+            here = here + bias[...]
+        score_slots[block % 2][span(chunk), :] = here
+        return jnp.maximum(run_max, here.reshape(SPAN // 8, 8, QB).max(axis=0))
+
+    def weigh(block, chunk, top, total):
+        terms = jnp.exp2(score_slots[block % 2][span(chunk), :] * SCALE - top)
+        weights[span(block * (block + 1) // 2 + chunk), :] = terms.astype(BF16)
         return total + terms.reshape(SPAN // 8, 8, QB).sum(axis=0)
 
-    total = lax.fori_loop(0, block + 1, second, jnp.zeros((8, QB), F32))
-    stats[pl.ds(block, 1), :] = top
-    stats[pl.ds(8 + block, 1), :] = total.sum(axis=0, keepdims=True)
+    lowest = jnp.full((8, QB), LOW, F32)
+    none = jnp.zeros((8, QB), F32)
+    run_max = lax.fori_loop(0, 7, lambda chunk, run: score(7, chunk, run, False), lowest)
+    run_max = score(7, 7, run_max, True)
+    for block in range(7, -1, -1):
+        top = run_max.max(axis=0, keepdims=True) * SCALE
+
+        def beside(chunk, carry, block=block, top=top):
+            total, run = carry
+            return (weigh(block, chunk, top, total), score(block - 1, chunk, run, False))
+
+        total, run_max = lax.fori_loop(0, block - 1, beside, (none, lowest))
+        if block > 0:
+            total = weigh(block, block - 1, top, total)
+            run_max = score(block - 1, block - 1, run_max, True)
+        total = weigh(block, block, top, total)
+        stats[block : block + 1, :] = top
+        stats[8 + block : 9 + block, :] = total.sum(axis=0, keepdims=True)
 
 
 def value_chunk(chunk, values, weights, totals):
@@ -215,8 +226,8 @@
     outer_in, turns, inner_in, inner_out, outer_out,
     halo, filt_send, prod_send, gate_send, filt_recv, prod_recv, gate_recv,
     hyena, home, wide, half, spec_x, spec_h, column,
-    query_all, key_all, value_all, scores, weights, stats, other_stats,
-    totals, own_part, part_send, part_recv, att_send, att_home, squares,
+    query_all, key_all, value_all, scores_even, scores_odd, bias, weights, stats, other_stats,
+    totals, own_part, part_send, part_recv, att_send, att_home, sum_own, sum_tp, sum_send, sum_home,
     send_sem, recv_sem, halo_send, halo_recv, part_out, part_in,
     load_sem, value_out_sem, value_in_sem,
 ):
@@ -395,6 +406,7 @@
     head_row = skip_gain[pl.ds(depth, 1), :]
     column[...] = jnp.broadcast_to(head_row, (DH, DH)).T
     skip_tile = column[rows16(my_block % 8), :]
+    bias[...] = visible_bias(core, across)
 
     wait_bytes(filt_recv.at[rest, :], recv_sem.at[0])
     spectrum(filt_recv, wide, half, spec_h, outer_in, turns, inner_in)
@@ -458,22 +470,10 @@
     wait_bytes(key_all.at[pl.ds(0, 3 * 1024), :], recv_sem.at[6])
     query_on.wait_recv()
 
-    def scoring(step, unused):
-        block = lax.rem(depth + step, 8)
-        attend_scores(
-            block, core, across, query_all, key_all, scores, weights, stats
-        )
-        return unused
-
-    lax.fori_loop(0, 8, scoring, 0)
+    attend_scores(core, query_all, key_all, (scores_even, scores_odd), bias, weights, stats)
     stats_out = remote(stats, other_stats, send_sem.at[9], recv_sem.at[9], sibling)
     stats_out.start()
 
-    for chunk in range(4):
-        wait_bytes(
-            value_all.at[pl.ds(0, 7 * PIECE), pl.ds(chunk * 1024, 1024)], value_in_sem.at[chunk]
-        )
-        value_chunk(chunk, value_all, weights, totals)
     stats_out.wait_recv()
 
     def part_copy(block):
@@ -485,13 +485,20 @@
             sibling,
         )
 
+    def share(block):
+        total = totals[block] * share_factor(block, stats, other_stats)
+        own_part[block] = total[:, :128]
+        part_send[block] = total[:, 128:].astype(BF16)
+        part_copy(block).start()
+
     def settle(block):
         part_copy(block).wait_recv()
-        whole = own_part[block] + part_recv[block].astype(F32)
-        att_send[pl.ds(pl.multiple_of(block * 128, 128), 128), :] = whole.T.astype(BF16)
-
-        for k in range(4):
-            goal = block * 4 + k
+        whole = (own_part[block] + part_recv[block].astype(F32)).astype(BF16).astype(F32)
+        att_send[pl.ds(block * 128, 128), :] = whole.T.astype(BF16)
+        sum_own[block : block + 1, :] = (whole * whole).sum(axis=0, keepdims=True)
+
+        for step in range(4):
+            goal = block * 4 + lax.rem(depth + step, 4)
             rows = pl.ds(pl.multiple_of(goal * 32, 32), 32)
 
             @pl.when(goal != pair)
@@ -508,48 +515,64 @@
             def _():
                 att_home[across_rows, my_cols] = att_send[rows, :]
 
-    def sharing(step, unused):
-        block = lax.rem(depth + step, 8)
-        total = totals[block] * share_factor(block, stats, other_stats)
-        own_part[block] = total[:, :128]
-        part_send[block] = total[:, 128:].astype(BF16)
-        part_copy(block).start()
-        return unused
-
-    lax.fori_loop(0, 8, sharing, 0)
-
-    def settling(step, unused):
-        settle(lax.rem(depth + step, 8))
-        return unused
-
-    lax.fori_loop(0, 8, settling, 0)
-
-    wait_bytes(home.at[rest, :], recv_sem.at[3])
-
-    def finish(head, unused):
-        cols = pl.ds(pl.multiple_of(head * DH, DH), DH)
-        hyena_out[:, cols] = home[cols, :].astype(F32).T.astype(BF16)
-        return unused
-
-    lax.fori_loop(0, 8, finish, 0)
-
-    wait_bytes(att_send.at[pl.ds(0, 31 * 32), :], recv_sem.at[10])
-    summed = jnp.zeros((TOK, DH), F32)
-    for head in range(8):
-        part = att_home[:, head * DH : (head + 1) * DH].astype(F32)
-        summed = summed + part * part
-    squares[tp] = jnp.broadcast_to(summed.T.sum(axis=0, keepdims=True), (8, TOK))
+    for chunk in range(4):
+        wait_bytes(
+            value_all.at[pl.ds(0, 7 * PIECE), pl.ds(chunk * 1024, 1024)], value_in_sem.at[chunk]
+        )
+        value_chunk(chunk, value_all, weights, totals)
+        share(2 * chunk)
+        share(2 * chunk + 1)
+        if chunk > 0:
+            settle(2 * chunk - 2)
+            settle(2 * chunk - 1)
+    settle(6)
+    settle(7)
+
+    sum_tp[tp] = sum_own[...]
     for step in range(1, 4):
         remote_tp(
-            squares.at[tp],
-            squares.at[tp],
+            sum_own,
+            sum_tp.at[tp],
             send_sem.at[11],
             recv_sem.at[11],
             lax.rem(tp + step, 4),
         ).start()
-    wait_bytes(squares.at[pl.ds(0, 3)], recv_sem.at[11])
-    mean = (squares[0] + squares[1] + squares[2] + squares[3]) * (1.0 / HC)
-    inverse = jnp.broadcast_to(lax.rsqrt(mean + 1e-05)[0:1, :], (TOK, TOK)).T
+    wait_bytes(sum_tp.at[pl.ds(0, 3)], recv_sem.at[11])
+    sum_send[...] = sum_tp[0] + sum_tp[1] + sum_tp[2] + sum_tp[3]
+
+    def sums_out(step, unused):
+        goal = lax.rem(pair + step, 32)
+        remote(
+            sum_send.at[pl.ds(goal // 4, 1), :],
+            sum_home.at[pl.ds(pair, 1), :],
+            send_sem.at[8],
+            recv_sem.at[8],
+            goal * 2 + core,
+        ).start()
+        return unused
+
+    lax.fori_loop(1, 32, sums_out, 0)
+    sum_home[pl.ds(pair, 1), :] = sum_send[pl.ds(pair // 4, 1), :]
+
+    wait_bytes(home.at[rest, :], recv_sem.at[3])
+
+    def finish(head, unused):
+        cols = pl.ds(pl.multiple_of(head * DH, DH), DH)
+        hyena_out[:, cols] = home[cols, :].astype(F32).T.astype(BF16)
+        return unused
+
+    lax.fori_loop(0, 8, finish, 0)
+
+    wait_bytes(sum_home.at[pl.ds(0, 31), :], recv_sem.at[8])
+    lane = lax.broadcasted_iota(jnp.int32, (1, TOK), 1)
+    mean = jnp.zeros((1, TOK), F32)
+    for group in range(4):
+        part = sum_home[8 * group : 8 * group + 8, :].sum(axis=0, keepdims=True)
+        part = pltpu.roll(jnp.broadcast_to(part, (8, TOK)), (group + 4 - pair % 4) * 32 % TOK, 1)
+        mean = jnp.where(lane // 32 == group, part[0:1, :], mean)
+    mean = mean * (1.0 / HC)
+    inverse = jnp.broadcast_to(lax.rsqrt(mean + 1e-05), (TOK, TOK)).T
+    wait_bytes(att_send.at[pl.ds(0, 31 * 32), :], recv_sem.at[10])
     for head in range(8):
         cols = slice(head * DH, (head + 1) * DH)
         part = att_home[:, cols].astype(F32)
@@ -569,7 +592,8 @@
     for block in range(8):
         part_copy(block).wait_send()
     wait_bytes(att_send.at[pl.ds(0, 31 * 32), :], send_sem.at[10])
-    wait_bytes(squares.at[pl.ds(0, 3)], send_sem.at[11])
+    wait_bytes(sum_tp.at[pl.ds(0, 3)], send_sem.at[11])
+    wait_bytes(sum_home.at[pl.ds(0, 31), :], send_sem.at[8])
 
     @pl.when(me < NC - 1)
     def _():
@@ -611,6 +635,8 @@
             pltpu.VMEM((4096, DH), BF16),
             pltpu.VMEM((DH, 4096), BF16),
             pltpu.VMEM((4096, QB), F32),
+            pltpu.VMEM((4096, QB), F32),
+            pltpu.VMEM((SPAN, QB), F32),
             pltpu.VMEM((36 * SPAN, QB), BF16),
             pltpu.VMEM((16, QB), F32),
             pltpu.VMEM((16, QB), F32),
@@ -620,12 +646,15 @@
             pltpu.VMEM((8, DH, 128), BF16),
             flat,
             pltpu.VMEM((TOK, 1024), BF16),
+            pltpu.VMEM((8, TOK), F32),
             pltpu.VMEM((4, 8, TOK), F32),
+            pltpu.VMEM((8, TOK), F32),
+            pltpu.VMEM((32, TOK), F32),
             dma((12,)), dma((12,)), dma((3,)), dma((3,)), dma((8,)), dma((8,)),
             dma((14,)), dma((4,)), dma((4,)),
         ],
         compiler_params=pltpu.CompilerParams(
-            collective_id=0, has_side_effects=True, vmem_limit_bytes=48 * 2**20
+            collective_id=0, has_side_effects=True, vmem_limit_bytes=63 * 2**20
         ),
     )(
         queries, key_vectors, stream_gate, stream_key, stream_value, short_filter, long_filter,

time: 89.2 us -> 76.1 us (0.85)
  the two profiles are of different devices: /device:TPU:2 before, /device:TPU:1 now
where the time goes in v4:
time: 76.1 us; the launch traced here: 76 us
  Pallas kernels  72.9 us (96%)
  local copies, waits for them, and re-layouts  2.42 us (3%)
    pallas_call x1, Pallas kernels, shards(): pl.pallas_call(kernel, out_shape=(shape, shape), in_specs=[pl.BlockSpec(m...  72.9 us
    unnamed x4, local copies, waits for them, and re-layouts  2.42 us

profile of v4, /device:TPU:1, one launch (start us, length us, event | category | flops | bytes accessed | tf_op | source)
XLA Modules:
  0.0 76.0 jit_solution(1494105350767931176)
XLA Ops:
  0.6 72.9 %shard_map.149 = (bf16[128,1024]{1,0:T(8,128)(2,1)}, bf16[128,1024]{1,0:T(8,128)(2,1)}) custom-call(bf16[128,1024]{1,0:T(8,128)(2,1)} %queries.1, bf16[128,1024]{1,0:T(8,128)(2,1)} %key_vectors.1, bf16[128,1024]{1,0:T(8,128)(2,1)} %gate_hbm.1, bf16[128,1024]{1,0:T(8,128)(2,1)} %key_hbm.1, bf16[128,1024]{1,0:T(8,128)(2,1)} %value_hbm.1, ...), custom_call_target="tpu_custom_call" | custom-call | tf_op jit(solution)/shard_map/pallas_call | solution.py:613
  73.6 0.0 copy-start
  73.6 1.7 %copy.18 = bf16[128,1024]{1,0:T(8,128)(2,1)} copy(bf16[128,1024]{1,0:T(8,128)(2,1)} %get-tuple-element.4) | data formatting | bytes 524288
  75.3 0.0 copy-done
  75.3 0.7 copy.19
Async XLA Ops:
  73.6 1.7 %copy-start = (bf16[128,1024]{1,0:T(8,128)(2,1)S(1)}, bf16[128,1024]{1,0:T(8,128)(2,1)}, u32[]{:S(2)}) copy-start(bf16[128,1024]{1,0:T(8,128)(2,1)} %get-tuple-element.5) | copy-start | bytes 786436

commit v5 on v4

--- a/solution.py
+++ b/solution.py
@@ -67,17 +67,6 @@
     )
 
 
-def remote_tp(src, dst, send_sem, recv_sem, dev):
-    return pltpu.make_async_remote_copy(
-        src_ref=src,
-        dst_ref=dst,
-        send_sem=send_sem,
-        recv_sem=recv_sem,
-        device_id={"tp": dev},
-        device_id_type=pl.DeviceIdType.MESH,
-    )
-
-
 def wait_bytes(ref, sem):
     pltpu.make_async_copy(ref, ref, sem).wait()
 
@@ -175,7 +164,7 @@
 
     lowest = jnp.full((8, QB), LOW, F32)
     none = jnp.zeros((8, QB), F32)
-    run_max = lax.fori_loop(0, 7, lambda chunk, run: score(7, chunk, run, False), lowest)
+    run_max = lax.fori_loop(0, 7, lambda chunk, run: score(7, chunk, run, False), lowest, unroll=7)
     run_max = score(7, 7, run_max, True)
     for block in range(7, -1, -1):
         top = run_max.max(axis=0, keepdims=True) * SCALE
@@ -184,7 +173,7 @@
             total, run = carry
             return (weigh(block, chunk, top, total), score(block - 1, chunk, run, False))
 
-        total, run_max = lax.fori_loop(0, block - 1, beside, (none, lowest))
+        total, run_max = lax.fori_loop(0, block - 1, beside, (none, lowest), unroll=2)
         if block > 0:
             total = weigh(block, block - 1, top, total)
             run_max = score(block - 1, block - 1, run_max, True)
@@ -227,9 +216,9 @@
     halo, filt_send, prod_send, gate_send, filt_recv, prod_recv, gate_recv,
     hyena, home, wide, half, spec_x, spec_h, column,
     query_all, key_all, value_all, scores_even, scores_odd, bias, weights, stats, other_stats,
-    totals, own_part, part_send, part_recv, att_send, att_home, sum_own, sum_tp, sum_send, sum_home,
+    totals, own_part, part_send, part_recv, att_send, att_home, sum_own, sum_home,
     send_sem, recv_sem, halo_send, halo_recv, part_out, part_in,
-    load_sem, value_out_sem, value_in_sem,
+    load_sem, value_out_sem, value_in_sem, plane_ready,
 ):
     me = lax.axis_index("ctx")
     tp = lax.axis_index("tp")
@@ -297,6 +286,13 @@
     loads[0].wait()
     filt_send[...] = long_filter[...].astype(BF16)
     pl.semaphore_wait(barrier, NC - 1 + 3)
+    for step in range(1, 4):
+        pl.semaphore_signal(
+            plane_ready,
+            inc=1,
+            device_id={"tp": lax.rem(tp + step, 4)},
+            device_id_type=pl.DeviceIdType.MESH,
+        )
 
     streams = (gate_hbm, key_hbm, value_hbm)
 
@@ -475,6 +471,7 @@
     stats_out.start()
 
     stats_out.wait_recv()
+    pl.semaphore_wait(plane_ready, 3)
 
     def part_copy(block):
         return remote(
@@ -491,13 +488,23 @@
         part_send[block] = total[:, 128:].astype(BF16)
         part_copy(block).start()
 
+    def sum_copy(block, goal, row):
+        return pltpu.make_async_remote_copy(
+            src_ref=sum_own.at[pl.ds(block, 1), :],
+            dst_ref=sum_home.at[pl.ds(tp * 32 + pair, 1), :],
+            send_sem=send_sem.at[8],
+            recv_sem=recv_sem.at[8],
+            device_id={"ctx": goal * 2 + core, "tp": row},
+            device_id_type=pl.DeviceIdType.MESH,
+        )
+
     def settle(block):
         part_copy(block).wait_recv()
         whole = (own_part[block] + part_recv[block].astype(F32)).astype(BF16).astype(F32)
         att_send[pl.ds(block * 128, 128), :] = whole.T.astype(BF16)
         sum_own[block : block + 1, :] = (whole * whole).sum(axis=0, keepdims=True)
 
-        for step in range(4):
+        def send(step, unused):
             goal = block * 4 + lax.rem(depth + step, 4)
             rows = pl.ds(pl.multiple_of(goal * 32, 32), 32)
 
@@ -510,10 +517,18 @@
                     recv_sem.at[10],
                     goal * 2 + core,
                 ).start()
+                sum_copy(block, goal, tp).start()
 
             @pl.when(goal == pair)
             def _():
                 att_home[across_rows, my_cols] = att_send[rows, :]
+                sum_home[pl.ds(tp * 32 + pair, 1), :] = sum_own[pl.ds(block, 1), :]
+
+            for other in range(1, 4):
+                sum_copy(block, goal, lax.rem(tp + other, 4)).start()
+            return unused
+
+        lax.fori_loop(0, 4, send, 0)
 
     for chunk in range(4):
         wait_bytes(
@@ -522,37 +537,8 @@
         value_chunk(chunk, value_all, weights, totals)
         share(2 * chunk)
         share(2 * chunk + 1)
-        if chunk > 0:
-            settle(2 * chunk - 2)
-            settle(2 * chunk - 1)
-    settle(6)
-    settle(7)
-
-    sum_tp[tp] = sum_own[...]
-    for step in range(1, 4):
-        remote_tp(
-            sum_own,
-            sum_tp.at[tp],
-            send_sem.at[11],
-            recv_sem.at[11],
-            lax.rem(tp + step, 4),
-        ).start()
-    wait_bytes(sum_tp.at[pl.ds(0, 3)], recv_sem.at[11])
-    sum_send[...] = sum_tp[0] + sum_tp[1] + sum_tp[2] + sum_tp[3]
-
-    def sums_out(step, unused):
-        goal = lax.rem(pair + step, 32)
-        remote(
-            sum_send.at[pl.ds(goal // 4, 1), :],
-            sum_home.at[pl.ds(pair, 1), :],
-            send_sem.at[8],
-            recv_sem.at[8],
-            goal * 2 + core,
-        ).start()
-        return unused
-
-    lax.fori_loop(1, 32, sums_out, 0)
-    sum_home[pl.ds(pair, 1), :] = sum_send[pl.ds(pair // 4, 1), :]
+        settle(2 * chunk)
+        settle(2 * chunk + 1)
 
     wait_bytes(home.at[rest, :], recv_sem.at[3])
 
@@ -563,12 +549,15 @@
 
     lax.fori_loop(0, 8, finish, 0)
 
-    wait_bytes(sum_home.at[pl.ds(0, 31), :], recv_sem.at[8])
+    wait_bytes(sum_home.at[pl.ds(0, 127), :], recv_sem.at[8])
     lane = lax.broadcasted_iota(jnp.int32, (1, TOK), 1)
     mean = jnp.zeros((1, TOK), F32)
     for group in range(4):
-        part = sum_home[8 * group : 8 * group + 8, :].sum(axis=0, keepdims=True)
-        part = pltpu.roll(jnp.broadcast_to(part, (8, TOK)), (group + 4 - pair % 4) * 32 % TOK, 1)
+        part = sum_home[8 * group : 8 * group + 8, :]
+        for row in range(1, 4):
+            part = part + sum_home[32 * row + 8 * group : 32 * row + 8 * group + 8, :]
+        part = jnp.broadcast_to(part.sum(axis=0, keepdims=True), (8, TOK))
+        part = pltpu.roll(part, (group + 4 - pair % 4) * 32 % TOK, 1)
         mean = jnp.where(lane // 32 == group, part[0:1, :], mean)
     mean = mean * (1.0 / HC)
     inverse = jnp.broadcast_to(lax.rsqrt(mean + 1e-05), (TOK, TOK)).T
@@ -592,8 +581,7 @@
     for block in range(8):
         part_copy(block).wait_send()
     wait_bytes(att_send.at[pl.ds(0, 31 * 32), :], send_sem.at[10])
-    wait_bytes(sum_tp.at[pl.ds(0, 3)], send_sem.at[11])
-    wait_bytes(sum_home.at[pl.ds(0, 31), :], send_sem.at[8])
+    wait_bytes(sum_home.at[pl.ds(0, 127), :], send_sem.at[8])
 
     @pl.when(me < NC - 1)
     def _():
@@ -647,11 +635,9 @@
             flat,
             pltpu.VMEM((TOK, 1024), BF16),
             pltpu.VMEM((8, TOK), F32),
-            pltpu.VMEM((4, 8, TOK), F32),
-            pltpu.VMEM((8, TOK), F32),
-            pltpu.VMEM((32, TOK), F32),
+            pltpu.VMEM((128, TOK), F32),
             dma((12,)), dma((12,)), dma((3,)), dma((3,)), dma((8,)), dma((8,)),
-            dma((14,)), dma((4,)), dma((4,)),
+            dma((14,)), dma((4,)), dma((4,)), pltpu.SemaphoreType.REGULAR,
         ],
         compiler_params=pltpu.CompilerParams(
             collective_id=0, has_side_effects=True, vmem_limit_bytes=63 * 2**20

time: 76.1 us -> 72.2 us (0.949)
  the two profiles are of different devices: /device:TPU:1 before, /device:TPU:4 now
where the time goes in v5:
time: 72.2 us; the launch traced here: 70.8 us
  Pallas kernels  67.8 us (94%)
  local copies, waits for them, and re-layouts  2.42 us (3%)
    pallas_call x1, Pallas kernels, shards(): pl.pallas_call(kernel, out_shape=(shape, shape), in_specs=[pl.BlockSpec(m...  67.8 us
    unnamed x4, local copies, waits for them, and re-layouts  2.42 us

profile of v5, /device:TPU:4, one launch (start us, length us, event | category | flops | bytes accessed | tf_op | source)
XLA Modules:
  0.0 70.8 jit_solution(15317217089300486429)
XLA Ops:
  0.6 67.8 %shard_map.149 = (bf16[128,1024]{1,0:T(8,128)(2,1)}, bf16[128,1024]{1,0:T(8,128)(2,1)}) custom-call(bf16[128,1024]{1,0:T(8,128)(2,1)} %queries.1, bf16[128,1024]{1,0:T(8,128)(2,1)} %key_vectors.1, bf16[128,1024]{1,0:T(8,128)(2,1)} %gate_hbm.1, bf16[128,1024]{1,0:T(8,128)(2,1)} %key_hbm.1, bf16[128,1024]{1,0:T(8,128)(2,1)} %value_hbm.1, ...), custom_call_target="tpu_custom_call" | custom-call | tf_op jit(solution)/shard_map/pallas_call | solution.py:601
  68.4 0.0 copy-start
  68.4 1.7 %copy.18 = bf16[128,1024]{1,0:T(8,128)(2,1)} copy(bf16[128,1024]{1,0:T(8,128)(2,1)} %get-tuple-element.4) | data formatting | bytes 524288
  70.1 0.0 copy-done
  70.1 0.7 copy.19
Async XLA Ops:
  68.4 1.7 %copy-start = (bf16[128,1024]{1,0:T(8,128)(2,1)S(1)}, bf16[128,1024]{1,0:T(8,128)(2,1)}, u32[]{:S(2)}) copy-start(bf16[128,1024]{1,0:T(8,128)(2,1)} %get-tuple-element.5) | copy-start | bytes 786436

commit v6 on v5

--- a/solution.py
+++ b/solution.py
@@ -208,15 +208,15 @@
 
 def kernel(
     queries, key_vectors, gate_hbm, key_hbm, value_hbm,
-    taps_hbm, filter_hbm, skip_hbm, gain_hbm,
+    taps_hbm, filter_hbm, skip_hbm,
     outer_in_hbm, turns_hbm, inner_in_hbm, inner_out_hbm, outer_out_hbm,
-    hyena_out, attn_out,
-    stream_gate, stream_key, stream_value, taps, long_filter, skip_gain, out_gain,
+    home_out, att_out, inverse_out,
+    stream_gate, stream_key, stream_value, taps, long_filter, skip_gain,
     outer_in, turns, inner_in, inner_out, outer_out,
     halo, filt_send, prod_send, gate_send, filt_recv, prod_recv, gate_recv,
     hyena, home, wide, half, spec_x, spec_h, column,
     query_all, key_all, value_all, scores_even, scores_odd, bias, weights, stats, other_stats,
-    totals, own_part, part_send, part_recv, att_send, att_home, sum_own, sum_home,
+    totals, own_part, part_send, part_recv, att_send, att_home, sum_own, sum_home, inverse,
     send_sem, recv_sem, halo_send, halo_recv, part_out, part_in,
     load_sem, value_out_sem, value_in_sem, plane_ready,
 ):
@@ -260,7 +260,6 @@
                 (inner_out_hbm, inner_out),
                 (outer_out_hbm, outer_out),
                 (skip_hbm, skip_gain),
-                (gain_hbm, out_gain),
             )
         )
     ]
@@ -354,7 +353,7 @@
         prod_send[cols, :] = product.T.astype(BF16)
         return unused
 
-    lax.fori_loop(0, 8, columns, 0)
+    lax.fori_loop(0, 8, columns, 0, unroll=2)
     scatter(prod_send, prod_recv, 1)
 
     def gate_columns(head, unused):
@@ -363,7 +362,7 @@
         gate_send[cols, :] = gate_feat.astype(F32).T.astype(BF16)
         return unused
 
-    lax.fori_loop(0, 8, gate_columns, 0)
+    lax.fori_loop(0, 8, gate_columns, 0, unroll=2)
     scatter(gate_send, gate_recv, 2)
 
     def query_out(step, unused):
@@ -450,7 +449,7 @@
         ).start()
         return unused
 
-    lax.fori_loop(1, NC, go_home, 0)
+    lax.fori_loop(1, NC, go_home, 0, unroll=9)
     home[rows16(my_block), :] = hyena[:, pl.ds(pl.multiple_of(my_slot * TOK, TOK), TOK)]
 
     wait_bytes(query_all.at[pl.ds(0, 31 * 32), :], recv_sem.at[5])
@@ -528,7 +527,7 @@
                 sum_copy(block, goal, lax.rem(tp + other, 4)).start()
             return unused
 
-        lax.fori_loop(0, 4, send, 0)
+        lax.fori_loop(0, 4, send, 0, unroll=True)
 
     for chunk in range(4):
         wait_bytes(
@@ -542,12 +541,8 @@
 
     wait_bytes(home.at[rest, :], recv_sem.at[3])
 
-    def finish(head, unused):
-        cols = pl.ds(pl.multiple_of(head * DH, DH), DH)
-        hyena_out[:, cols] = home[cols, :].astype(F32).T.astype(BF16)
-        return unused
-
-    lax.fori_loop(0, 8, finish, 0)
+    home_copy = pltpu.make_async_copy(home, home_out, load_sem.at[14])
+    home_copy.start()
 
     wait_bytes(sum_home.at[pl.ds(0, 127), :], recv_sem.at[8])
     lane = lax.broadcasted_iota(jnp.int32, (1, TOK), 1)
@@ -560,12 +555,12 @@
         part = pltpu.roll(part, (group + 4 - pair % 4) * 32 % TOK, 1)
         mean = jnp.where(lane // 32 == group, part[0:1, :], mean)
     mean = mean * (1.0 / HC)
-    inverse = jnp.broadcast_to(lax.rsqrt(mean + 1e-05), (TOK, TOK)).T
+    inverse[...] = jnp.broadcast_to(lax.rsqrt(mean + 1e-05), (8, TOK))
+    inverse_copy = pltpu.make_async_copy(inverse, inverse_out, load_sem.at[15])
+    inverse_copy.start()
     wait_bytes(att_send.at[pl.ds(0, 31 * 32), :], recv_sem.at[10])
-    for head in range(8):
-        cols = slice(head * DH, (head + 1) * DH)
-        part = att_home[:, cols].astype(F32)
-        attn_out[:, cols] = (part * inverse * out_gain[0:1, cols]).astype(BF16)
+    att_copy = pltpu.make_async_copy(att_home, att_out, load_sem.at[16])
+    att_copy.start()
 
     for index, send in enumerate((filt_send, prod_send, gate_send, home)):
         wait_bytes(send.at[rest, :], send_sem.at[index])
@@ -583,10 +578,41 @@
     wait_bytes(att_send.at[pl.ds(0, 31 * 32), :], send_sem.at[10])
     wait_bytes(sum_home.at[pl.ds(0, 127), :], send_sem.at[8])
 
+    home_copy.wait()
+    inverse_copy.wait()
+    att_copy.wait()
+
     @pl.when(me < NC - 1)
     def _():
         for which, stream in enumerate(streams):
             wait_bytes(stream.at[pl.ds(TOK - 16, 16), :], halo_send.at[which])
+
+
+def finish_kernel(
+    home_hbm, att_hbm, inverse_hbm, gain_hbm, hyena_out, attn_out,
+    home, attended, inverse, out_gain, sem,
+):
+    loads = [
+        pltpu.make_async_copy(src, dst, sem.at[index])
+        for index, (src, dst) in enumerate(
+            (
+                (home_hbm, home),
+                (att_hbm, attended),
+                (inverse_hbm, inverse),
+                (gain_hbm, out_gain),
+            )
+        )
+    ]
+    for load in loads:
+        load.start()
+    for load in loads:
+        load.wait()
+    column = jnp.broadcast_to(inverse[0:1, :], (TOK, TOK)).T
+    for head in range(8):
+        cols = slice(head * DH, (head + 1) * DH)
+        hyena_out[:, cols] = home[cols, :].astype(F32).T.astype(BF16)
+        part = attended[:, cols].astype(F32)
+        attn_out[:, cols] = (part * column * out_gain[0:1, cols]).astype(BF16)
 
 
 def shards(
@@ -598,17 +624,20 @@
     dma = pltpu.SemaphoreType.DMA
     constants = dft_constants()
     shape = jax.ShapeDtypeStruct(stream_gate.shape, BF16)
-    return pl.pallas_call(
+    home, attended, inverse = pl.pallas_call(
         kernel,
-        out_shape=(shape, shape),
-        in_specs=[pl.BlockSpec(memory_space=pltpu.HBM)] * 14,
-        out_specs=(vmem, vmem),
+        out_shape=(
+            jax.ShapeDtypeStruct((NC * PIECE, TOK), BF16),
+            shape,
+            jax.ShapeDtypeStruct((8, TOK), F32),
+        ),
+        in_specs=[pl.BlockSpec(memory_space=pltpu.HBM)] * 13,
+        out_specs=(pl.BlockSpec(memory_space=pltpu.HBM),) * 3,
         scratch_shapes=[
             *[pltpu.VMEM((TOK, 1024), BF16)] * 3,
             pltpu.VMEM((3, 3, 1024), F32),
             pltpu.VMEM((1024, TOK), F32),
             pltpu.VMEM((8, DH), F32),
-            pltpu.VMEM((1, 1024), F32),
             *[pltpu.VMEM(c.shape, c.dtype) for c in constants],
             pltpu.VMEM((3, 16, 1024), BF16),
             flat, flat, flat, flat, flat, flat,
@@ -636,16 +665,31 @@
             pltpu.VMEM((TOK, 1024), BF16),
             pltpu.VMEM((8, TOK), F32),
             pltpu.VMEM((128, TOK), F32),
+            pltpu.VMEM((8, TOK), F32),
             dma((12,)), dma((12,)), dma((3,)), dma((3,)), dma((8,)), dma((8,)),
-            dma((14,)), dma((4,)), dma((4,)), pltpu.SemaphoreType.REGULAR,
+            dma((17,)), dma((4,)), dma((4,)), pltpu.SemaphoreType.REGULAR,
         ],
         compiler_params=pltpu.CompilerParams(
             collective_id=0, has_side_effects=True, vmem_limit_bytes=63 * 2**20
         ),
     )(
         queries, key_vectors, stream_gate, stream_key, stream_value, short_filter, long_filter,
-        skip_gain.reshape(8, DH), out_gain.reshape(1, 1024), *constants,
+        skip_gain.reshape(8, DH), *constants,
     )
+    return pl.pallas_call(
+        finish_kernel,
+        out_shape=(shape, shape),
+        in_specs=[pl.BlockSpec(memory_space=pltpu.HBM)] * 4,
+        out_specs=(vmem, vmem),
+        scratch_shapes=[
+            flat,
+            pltpu.VMEM((TOK, 1024), BF16),
+            pltpu.VMEM((8, TOK), F32),
+            pltpu.VMEM((1, 1024), F32),
+            dma((4,)),
+        ],
+        compiler_params=pltpu.CompilerParams(vmem_limit_bytes=63 * 2**20),
+    )(home, attended, inverse, out_gain.reshape(1, 1024))
 
 
 def solution(mesh):

time: 72.2 us -> 71.4 us (0.989)
  local copies, waits for them, and re-layouts: 2.42 us -> 0 us
  Pallas kernels: 67.8 us -> 69.6 us
    unnamed x4 -> x0, local copies, waits for them, and re-layouts: 2.42 us -> none
    pallas_call x1 -> x2, Pallas kernels: 67.8 us -> 69.6 us  [the longest x1 67.6 us: shards(): pl.pallas_call(kernel, out_shape=(jax.ShapeDtypeStruct((NC * PIECE, TOK),...]
where the time goes in v6:
time: 71.4 us; the launch traced here: 70.2 us
  Pallas kernels  69.6 us (97%)
    pallas_call x1, Pallas kernels, shards(): pl.pallas_call(kernel, out_shape=(jax.ShapeDtypeStruct((NC * PIECE, TOK),...  67.6 us
    pallas_call x1, Pallas kernels, shards(): pl.pallas_call(finish_kernel, out_shape=(shape, shape), in_specs=[pl.Bloc...  1.99 us

profile of v6, /device:TPU:4, one launch (start us, length us, event | category | flops | bytes accessed | tf_op | source)
XLA Modules:
  0.0 70.2 jit_solution(1624902551839462865)
XLA Ops:
  0.6 67.6 %shard_map.149 = (bf16[1024,128]{1,0:T(8,128)(2,1)}, bf16[128,1024]{1,0:T(8,128)(2,1)}, f32[8,128]{1,0:T(8,128)}) custom-call(bf16[128,1024]{1,0:T(8,128)(2,1)} %queries.1, bf16[128,1024]{1,0:T(8,128)(2,1)} %key_vectors.1, bf16[128,1024]{1,0:T(8,128)(2,1)} %gate_hbm.1, bf16[128,1024]{1,0:T(8,128)(2,1)} %key_hbm.1, bf16[128,1024]{1,0:T(8,128)(2,1)} %value_hbm.1, ...), custom_call_target="tpu_custom_call" | custom-call | tf_op jit(solution)/shard_map/pallas_call | solution.py:627
  68.2 2.0 %shard_map.150 = (bf16[128,1024]{1,0:T(8,128)(2,1)}, bf16[128,1024]{1,0:T(8,128)(2,1)}) custom-call(bf16[1024,128]{1,0:T(8,128)(2,1)} %get-tuple-element.5.home_hbm, bf16[128,1024]{1,0:T(8,128)(2,1)} %get-tuple-element.6.att_hbm, f32[8,128]{1,0:T(8,128)} %get-tuple-element.7.inverse_hbm, f32[1,1024]{1,0:T(1,128)} %bitcast.3), custom_call_target="tpu_custom_call" | custom-call | tf_op jit(solution)/shard_map/pallas_call | solution.py:679

commit v7 on v6

--- a/solution.py
+++ b/solution.py
@@ -590,7 +590,7 @@
 
 def finish_kernel(
     home_hbm, att_hbm, inverse_hbm, gain_hbm, hyena_out, attn_out,
-    home, attended, inverse, out_gain, sem,
+    home, attended, inverse, out_gain, hyena_here, attn_here, sem,
 ):
     loads = [
         pltpu.make_async_copy(src, dst, sem.at[index])
@@ -605,14 +605,23 @@
     ]
     for load in loads:
         load.start()
-    for load in loads:
+    loads[0].wait()
+    for head in range(8):
+        cols = slice(head * DH, (head + 1) * DH)
+        hyena_here[:, cols] = home[cols, :].astype(F32).T.astype(BF16)
+    hyena_write = pltpu.make_async_copy(hyena_here, hyena_out, sem.at[4])
+    hyena_write.start()
+    for load in loads[1:]:
         load.wait()
     column = jnp.broadcast_to(inverse[0:1, :], (TOK, TOK)).T
     for head in range(8):
         cols = slice(head * DH, (head + 1) * DH)
-        hyena_out[:, cols] = home[cols, :].astype(F32).T.astype(BF16)
         part = attended[:, cols].astype(F32)
-        attn_out[:, cols] = (part * column * out_gain[0:1, cols]).astype(BF16)
+        attn_here[:, cols] = (part * column * out_gain[0:1, cols]).astype(BF16)
+    attn_write = pltpu.make_async_copy(attn_here, attn_out, sem.at[5])
+    attn_write.start()
+    hyena_write.wait()
+    attn_write.wait()
 
 
 def shards(
@@ -680,13 +689,15 @@
         finish_kernel,
         out_shape=(shape, shape),
         in_specs=[pl.BlockSpec(memory_space=pltpu.HBM)] * 4,
-        out_specs=(vmem, vmem),
+        out_specs=(pl.BlockSpec(memory_space=pltpu.HBM),) * 2,
         scratch_shapes=[
             flat,
             pltpu.VMEM((TOK, 1024), BF16),
             pltpu.VMEM((8, TOK), F32),
             pltpu.VMEM((1, 1024), F32),
-            dma((4,)),
+            pltpu.VMEM((TOK, 1024), BF16),
+            pltpu.VMEM((TOK, 1024), BF16),
+            dma((6,)),
         ],
         compiler_params=pltpu.CompilerParams(vmem_limit_bytes=63 * 2**20),
     )(home, attended, inverse, out_gain.reshape(1, 1024))

time: 71.4 us -> 71.4 us (level)
  no operation moved by 1% of the time
where the time goes in v7:
time: 71.4 us; the launch traced here: 70.2 us
  Pallas kernels  69.6 us (97%)
    pallas_call x1, Pallas kernels, shards(): pl.pallas_call(kernel, out_shape=(jax.ShapeDtypeStruct((NC * PIECE, TOK),...  67.6 us
    pallas_call x1, Pallas kernels, shards(): pl.pallas_call(finish_kernel, out_shape=(shape, shape), in_specs=[pl.Bloc...  1.99 us

profile of v7, /device:TPU:4, one launch (start us, length us, event | category | flops | bytes accessed | tf_op | source)
XLA Modules:
  0.0 70.2 jit_solution(5103886733599953437)
XLA Ops:
  0.6 67.6 %shard_map.149 = (bf16[1024,128]{1,0:T(8,128)(2,1)}, bf16[128,1024]{1,0:T(8,128)(2,1)}, f32[8,128]{1,0:T(8,128)}) custom-call(bf16[128,1024]{1,0:T(8,128)(2,1)} %queries.1, bf16[128,1024]{1,0:T(8,128)(2,1)} %key_vectors.1, bf16[128,1024]{1,0:T(8,128)(2,1)} %gate_hbm.1, bf16[128,1024]{1,0:T(8,128)(2,1)} %key_hbm.1, bf16[128,1024]{1,0:T(8,128)(2,1)} %value_hbm.1, ...), custom_call_target="tpu_custom_call" | custom-call | tf_op jit(solution)/shard_map/pallas_call | solution.py:636
  68.2 2.0 %shard_map.150 = (bf16[128,1024]{1,0:T(8,128)(2,1)}, bf16[128,1024]{1,0:T(8,128)(2,1)}) custom-call(bf16[1024,128]{1,0:T(8,128)(2,1)} %get-tuple-element.5.home_hbm, bf16[128,1024]{1,0:T(8,128)(2,1)} %get-tuple-element.6.att_hbm, f32[8,128]{1,0:T(8,128)} %get-tuple-element.7.inverse_hbm, f32[1,1024]{1,0:T(1,128)} %bitcast.3), custom_call_target="tpu_custom_call" | custom-call | tf_op jit(solution)/shard_map/pallas_call | solution.py:688
